TPU v7x, 32 devices: a whole 2x2x4 slice. The times are simulated.
32 devices in a mesh: dp: 2 (over core), expert: 16 (over z, y, x), tensor: 1.
Axes of the slice: x: 2, y: 2, z: 4, core: 2. Of those that a mesh axis runs over, the one named last changes fastest.
Arguments:
- tokens: bfloat16 [2048, 2048], P(('dp', 'expert'), 'tensor'), may hold values from -6 to 6
- expert_ids: int32 [2048, 6], P(('dp', 'expert')), may hold values from 0 to 15, all different within a row; in each aligned block of 64 rows (0 to 63, 64 to 127, ...) at most 32 rows name the same one
- route_weights: float32 [2048, 6], P(('dp', 'expert')), may hold values from 0.1 to 1
- w_gate: bfloat16 [16, 1408, 2048], P('expert', 'tensor'), may hold values from -0.125 to 0.125
- w_up: bfloat16 [16, 1408, 2048], P('expert', 'tensor'), may hold values from -0.125 to 0.125
- w_down: bfloat16 [16, 1408, 2048], P('expert', 'tensor'), may hold values from -0.15625 to 0.15625
- out_grad: bfloat16 [2048, 2048], P(('dp', 'expert'), 'tensor'), may hold values from -6 to 6
Outputs:
- layer_out: bfloat16 [2048, 2048], P(('dp', 'expert'), 'tensor')
- grad_tokens: bfloat16 [2048, 2048], P(('dp', 'expert'), 'tensor')
- grad_weights: float32 [2048, 6], P(('dp', 'expert'))
- grad_gate: bfloat16 [16, 1408, 2048], P('expert', 'tensor')
- grad_up: bfloat16 [16, 1408, 2048], P('expert', 'tensor')
- grad_down: bfloat16 [16, 1408, 2048], P('expert', 'tensor')
Inputs may be any that keep to these rules, and one draw needn't show every extreme that they name: `expert_ids`: each row names 6 different experts. In each aligned block of 64 rows no expert is named more than 32 times, a bound that some block reaches.
All inputs are finite; a program needn't handle non-finite values.
Results may differ from a plain program's by a relative error of at most 0.014.
Values may be sent and summed in bfloat16 or wider, within the bound.
A program may use at most 128 MiB of HBM per device.

v0:
```python
import jax
import jax.numpy as jnp
from jax import lax
from jax.sharding import PartitionSpec as P


def build_slots(block_ids, capacity, experts):
    onehot = (block_ids[:, None] == jnp.arange(experts, dtype=jnp.int32)[None, :]).astype(jnp.int32)
    before = jnp.cumsum(onehot, axis=0) - onehot
    position = jnp.sum(before * onehot, axis=1)
    slot_index = block_ids * capacity + position
    count = block_ids.shape[0]
    lookup = (
        jnp.full((experts * capacity,), -1, jnp.int32)
        .at[slot_index]
        .set(jnp.arange(count, dtype=jnp.int32))
    )
    return (slot_index, lookup)


def rounded(value):
    return lax.optimization_barrier(value.astype(jnp.bfloat16)).astype(jnp.float32)


def contract_rows(left, right):
    return lax.dot_general(
        left, right, (((0,), (0,)), ((), ())), preferred_element_type=jnp.float32
    )


def contract_cols(left, right):
    return lax.dot_general(
        left, right, (((1,), (1,)), ((), ())), preferred_element_type=jnp.float32
    )


def bring_back(part, slot_rows, scales, direction):
    summed = lax.psum_scatter(
        lax.optimization_barrier(part).astype(jnp.float32).astype(jnp.bfloat16),
        "tensor",
        scatter_dimension=1,
        tiled=True,
    ).astype(jnp.float32)
    returned = lax.all_to_all(
        summed.astype(jnp.bfloat16), "expert", split_axis=0, concat_axis=0, tiled=True
    ).astype(summed.dtype)
    picked = jnp.take(returned, slot_rows, axis=0)
    if scales is None:
        total = jnp.sum(picked, axis=1)
    else:
        total = jnp.sum(scales[:, :, None] * picked, axis=1)
    dots = None
    if direction is not None:
        dots = jnp.sum(direction.astype(jnp.float32)[:, None, :] * picked, axis=2)
    return (total, dots)


def body(tokens, expert_ids, route_weights, w_gate, w_up, w_down, out_grad):
    experts = lax.axis_size("expert")
    tok_rows, choose = expert_ids.shape
    capacity = tok_rows * 8 // experts
    slot_index, lookup = build_slots(expert_ids.reshape(-1), capacity, experts)
    filled = lookup >= 0
    pair_index = jnp.where(filled, lookup, 0)
    source_row = jnp.where(filled, pair_index // choose, tok_rows)
    slot_weight = jnp.where(
        filled, route_weights.reshape(-1)[pair_index], jnp.zeros((), jnp.float32)
    )
    slot_rows = slot_index.reshape(tok_rows, choose)

    def select_rows(rows):
        padded = jnp.concatenate([rows, jnp.zeros((1, rows.shape[1]), rows.dtype)], axis=0)
        return jnp.take(padded, source_row, axis=0)

    gathered, gathered_dy = (
        lax.all_gather(tokens, "tensor", axis=1, tiled=True),
        lax.all_gather(out_grad, "tensor", axis=1, tiled=True),
    )
    sent_rows = select_rows(gathered)
    sent_grads = (slot_weight[:, None] * select_rows(gathered_dy).astype(jnp.float32)).astype(
        jnp.bfloat16
    )
    sent_rows, sent_grads = (sent_rows, sent_grads)
    expert_rows, expert_grads = (
        lax.all_to_all(sent_rows, "expert", split_axis=0, concat_axis=0, tiled=True),
        lax.all_to_all(sent_grads, "expert", split_axis=0, concat_axis=0, tiled=True),
    )
    gate_matrix = w_gate[0]
    up_matrix = w_up[0]
    down_matrix = w_down[0]
    gate_value = contract_cols(expert_rows, gate_matrix)
    up_value = contract_cols(expert_rows, up_matrix)
    hidden = (jax.nn.silu(gate_value) * up_value).astype(jnp.bfloat16)
    part = jnp.dot(hidden, down_matrix, preferred_element_type=jnp.float32).astype(jnp.bfloat16)
    grad_hidden = contract_cols(expert_grads, down_matrix)
    sigma = jax.nn.sigmoid(gate_value)
    gate_rows = (grad_hidden * up_value * sigma * (1.0 + gate_value * (1.0 - sigma))).astype(
        jnp.bfloat16
    )
    up_rows = (grad_hidden * jax.nn.silu(gate_value)).astype(jnp.bfloat16)
    grad_part = (
        jnp.dot(gate_rows, gate_matrix, preferred_element_type=jnp.float32)
        + jnp.dot(up_rows, up_matrix, preferred_element_type=jnp.float32)
    ).astype(jnp.bfloat16)
    gate_term = rounded(contract_rows(gate_rows, expert_rows))
    up_term = rounded(contract_rows(up_rows, expert_rows))
    down_term = rounded(contract_rows(hidden, expert_grads))
    gate_sum, up_sum, down_sum = (
        lax.psum(gate_term.astype(jnp.bfloat16), "dp").astype(jnp.float32),
        lax.psum(up_term.astype(jnp.bfloat16), "dp").astype(jnp.float32),
        lax.psum(down_term.astype(jnp.bfloat16), "dp").astype(jnp.float32),
    )
    layer_total, dots = bring_back(part, slot_rows, route_weights, out_grad)
    grad_total, nothing = bring_back(grad_part, slot_rows, None, None)
    weight_dots = lax.psum(dots, "tensor")
    return (
        layer_total.astype(jnp.bfloat16),
        grad_total.astype(jnp.bfloat16),
        weight_dots,
        gate_sum.astype(jnp.bfloat16)[None],
        up_sum.astype(jnp.bfloat16)[None],
        down_sum.astype(jnp.bfloat16)[None],
    )


def solution(mesh):
    placed = (
        P(("dp", "expert"), "tensor"),
        P(("dp", "expert"), None),
        P(("dp", "expert"), None),
        P("expert", "tensor", None),
        P("expert", "tensor", None),
        P("expert", "tensor", None),
        P(("dp", "expert"), "tensor"),
    )
    return jax.shard_map(
        body,
        mesh=mesh,
        in_specs=placed,
        out_specs=(
            P(("dp", "expert"), "tensor"),
            P(("dp", "expert"), "tensor"),
            P(("dp", "expert"), None),
            P("expert", "tensor", None),
            P("expert", "tensor", None),
            P("expert", "tensor", None),
        ),
        check_vma=False,
    )
```

profile of v0, /device:TPU:12, one launch (start us, length us, event | category | flops | bytes accessed | tf_op | source)
XLA Modules:
  0.0 312.5 jit_solution(5441757963761513804)
XLA Ops:
  10.4 2.9 scatter_custom_fusion
  18.4 7.3 %all-to-all-start = ((bf16[16,32,2048]{2,1,0:T(8,128)(2,1)}), bf16[16,32,2048]{2,1,0:T(8,128)(2,1)}, u32[]{:S(2)}, u32[]{:S(2)}) async-start(bf16[16,32,2048]{2,1,0:T(8,128)(2,1)} %bitcast.69), calls=%async_computation | async-start | bytes 4194304 | tf_op jit(solution)/shard_map/all_to_all | solution.py:85
  28.5 3.5 %gather_fusion = f32[512]{0:T(512)S(1)} fusion(f32[384]{0:T(512)S(1)} %reshape.89, s32[1024]{0:T(1024)S(1)} %pad_clamp_fusion), kind=kCustom, calls=%fused_computation.4 | custom fusion | bytes 6144 | tf_op jit(solution)/shard_map/gather | solution.py:67
  33.9 40.1 %all-to-all-done = bf16[16,32,2048]{2,1,0:T(8,128)(2,1)} async-done(((bf16[16,32,2048]{2,1,0:T(8,128)(2,1)}), bf16[16,32,2048]{2,1,0:T(8,128)(2,1)}, u32[]{:S(2)}, u32[]{:S(2)}) %all-to-all-start) | async-done | bytes 2097184 | tf_op jit(solution)/shard_map/all_to_all | solution.py:85
  73.9 4.9 %all-to-all-start.2 = ((bf16[16,32,2048]{2,1,0:T(8,128)(2,1)}), bf16[16,32,2048]{2,1,0:T(8,128)(2,1)S(1)}, u32[]{:S(2)}, u32[]{:S(2)}) async-start(bf16[16,32,2048]{2,1,0:T(8,128)(2,1)} %bitcast.70), calls=%async_computation.2 | async-start | bytes 4194304 | tf_op jit(solution)/shard_map/all_to_all | solution.py:86
  79.1 8.3 %fusion.6 = f32[512,1408]{1,0:T(8,128)} fusion(bf16[512,2048]{1,0:T(8,128)(2,1)} %bitcast.2, bf16[1,1408,2048]{2,1,0:T(8,128)(2,1)} %param.15), kind=kOutput, calls=%fused_computation.15 | convolution fusion | flops 2952790016 | bytes 10747904 | tf_op jit(solution)/shard_map/dot_general | solution.py:32
  87.4 39.0 %all-to-all-done.2 = bf16[16,32,2048]{2,1,0:T(8,128)(2,1)S(1)} async-done(((bf16[16,32,2048]{2,1,0:T(8,128)(2,1)}), bf16[16,32,2048]{2,1,0:T(8,128)(2,1)S(1)}, u32[]{:S(2)}, u32[]{:S(2)}) %all-to-all-start.2) | async-done | bytes 2097184 | tf_op jit(solution)/shard_map/all_to_all | solution.py:86
  126.4 5.9 %fusion = f32[512,1408]{1,0:T(8,128)S(1)} fusion(bf16[512,2048]{1,0:T(8,128)(2,1)S(1)} %bitcast.77, bf16[1,1408,2048]{2,1,0:T(8,128)(2,1)} %param.16), kind=kOutput, calls=%fused_computation.9 | convolution fusion | flops 2952790016 | bytes 10747904 | tf_op jit(solution)/shard_map/dot_general | solution.py:32
  132.4 7.9 %multiply_convert_fusion.2 = (bf16[512,1408]{1,0:T(8,128)(2,1)S(1)}, bf16[512,1408]{1,0:T(8,128)(2,1)S(1)}, bf16[512,1408]{1,0:T(8,128)(2,1)S(1)}) fusion(f32[512,1408]{1,0:T(8,128)S(1)} %fusion, f32[512,1408]{1,0:T(8,128)S(1)} %copy-done.4, bf16[512,2048]{1,0:T(8,128)(2,1)} %bitcast.2, bf16[1,1408,2048]{2,1,0:T(8,128)(2,1)} %param.14), kind=kOutput, calls=%fused_computation.28 | convolution fusion | flops 2963603456 | bytes 17956864 | tf_op jit(solution)/shard_map/dot_general | solution.py:32
  140.3 5.0 %convolution_convert_fusion = bf16[1408,2048]{1,0:T(8,128)(2,1)} fusion(bf16[512,1408]{1,0:T(8,128)(2,1)S(1)} %get-tuple-element.32, bf16[512,2048]{1,0:T(8,128)(2,1)S(1)} %bitcast.78), kind=kOutput, calls=%fused_computation.6 | convolution fusion | flops 2955673600 | bytes 9306112 | tf_op jit(solution)/shard_map/dot_general | solution.py:26
  145.4 7.3 %convolution_convert_fusion.2 = bf16[1408,2048]{1,0:T(8,128)(2,1)} fusion(bf16[512,1408]{1,0:T(8,128)(2,1)S(1)} %get-tuple-element.30, bf16[512,2048]{1,0:T(8,128)(2,1)} %bitcast.2), kind=kOutput, calls=%fused_computation.8 | convolution fusion | flops 2955673600 | bytes 9306112 | tf_op jit(solution)/shard_map/dot_general | solution.py:26
  152.7 7.3 %convolution_convert_fusion.1 = bf16[1408,2048]{1,0:T(8,128)(2,1)} fusion(bf16[512,1408]{1,0:T(8,128)(2,1)S(1)} %get-tuple-element.31, bf16[512,2048]{1,0:T(8,128)(2,1)} %bitcast.2), kind=kOutput, calls=%fused_computation.7 | convolution fusion | flops 2955673600 | bytes 9306112 | tf_op jit(solution)/shard_map/dot_general | solution.py:26
  161.4 7.2 %fusion.14 = bf16[512,2048]{1,0:T(8,128)(2,1)} fusion(bf16[512,1408]{1,0:T(8,128)(2,1)S(1)} %copy-done.9, bf16[1,1408,2048]{2,1,0:T(8,128)(2,1)} %param.16), kind=kOutput, calls=%fused_computation.26 | convolution fusion | flops 2953838592 | bytes 9306112 | tf_op jit(solution)/shard_map/dot_general | solution.py:94
  168.6 4.7 %all-to-all-start.1 = ((bf16[16,32,2048]{2,1,0:T(8,128)(2,1)}), bf16[16,32,2048]{2,1,0:T(8,128)(2,1)S(1)}, u32[]{:S(2)}, u32[]{:S(2)}) async-start(bf16[16,32,2048]{2,1,0:T(8,128)(2,1)} %bitcast.79), calls=%async_computation.1 | async-start | bytes 4194304 | tf_op jit(solution)/shard_map/all_to_all | solution.py:44
  173.3 7.0 %fusion.4 = f32[512,2048]{1,0:T(8,128)S(1)} fusion(bf16[512,1408]{1,0:T(8,128)(2,1)} %copy-done.7, bf16[1,1408,2048]{2,1,0:T(8,128)(2,1)} %param.15), kind=kOutput, calls=%fused_computation.13 | convolution fusion | flops 2952790016 | bytes 11403264 | tf_op jit(solution)/shard_map/dot_general | solution.py:103
  180.3 8.5 %add_convert_fusion = bf16[512,2048]{1,0:T(8,128)(2,1)} fusion(f32[512,2048]{1,0:T(8,128)S(1)} %fusion.4, bf16[512,1408]{1,0:T(8,128)(2,1)S(1)} %copy-done.6, bf16[1,1408,2048]{2,1,0:T(8,128)(2,1)} %param.14), kind=kOutput, calls=%fused_computation.23 | convolution fusion | flops 2954887168 | bytes 13500416 | tf_op jit(solution)/shard_map/dot_general | solution.py:102
  188.9 32.0 %all-to-all-done.1 = bf16[16,32,2048]{2,1,0:T(8,128)(2,1)S(1)} async-done(((bf16[16,32,2048]{2,1,0:T(8,128)(2,1)}), bf16[16,32,2048]{2,1,0:T(8,128)(2,1)S(1)}, u32[]{:S(2)}, u32[]{:S(2)}) %all-to-all-start.1) | async-done | bytes 2097184 | tf_op jit(solution)/shard_map/all_to_all | solution.py:44
  220.9 4.7 %all-to-all-start.3 = ((bf16[16,32,2048]{2,1,0:T(8,128)(2,1)}), bf16[16,32,2048]{2,1,0:T(8,128)(2,1)}, u32[]{:S(2)}, u32[]{:S(2)}) async-start(bf16[16,32,2048]{2,1,0:T(8,128)(2,1)} %bitcast.76), calls=%async_computation.3 | async-start | bytes 4194304 | tf_op jit(solution)/shard_map/all_to_all | solution.py:44
  229.7 6.5 %gather_fusion.2 = f32[384,2048]{1,0:T(8,128)S(1)} fusion(f32[512,2048]{1,0:T(8,128)} %bitcast_convert_fusion.1, s32[1024]{0:T(1024)S(1)} %pad_clamp_fusion.1), kind=kCustom, calls=%fused_computation.1.clone | custom fusion | bytes 6292992 | tf_op jit(solution)/shard_map/jit(_take)/gather | solution.py:47
  238.4 34.9 %all-to-all-done.3 = bf16[16,32,2048]{2,1,0:T(8,128)(2,1)} async-done(((bf16[16,32,2048]{2,1,0:T(8,128)(2,1)}), bf16[16,32,2048]{2,1,0:T(8,128)(2,1)}, u32[]{:S(2)}, u32[]{:S(2)}) %all-to-all-start.3) | async-done | bytes 2097184 | tf_op jit(solution)/shard_map/all_to_all | solution.py:44
  273.3 4.1 %bitcast_convert_fusion = f32[512,2048]{1,0:T(8,128)} fusion(bf16[16,32,2048]{2,1,0:T(8,128)(2,1)} %all-to-all-done.3), kind=kLoop, calls=%fused_computation.32 | loop fusion | flops 1048576 | bytes 6291456 | tf_op jit(solution)/shard_map/convert_element_type | solution.py:46
  277.4 6.5 %gather_fusion.4 = f32[384,2048]{1,0:T(8,128)S(1)} fusion(f32[512,2048]{1,0:T(8,128)} %bitcast_convert_fusion, s32[1024]{0:T(1024)S(1)} %pad_clamp_fusion.1), kind=kCustom, calls=%fused_computation.3.clone | custom fusion | bytes 6292992 | tf_op jit(solution)/shard_map/jit(_take)/gather | solution.py:47
  286.2 6.9 %multiply_reduce_fusion = (f32[64,6]{1,0:T(8,128)S(1)}, bf16[64,2048]{1,0:T(8,128)(2,1)}, bf16[64,2048]{1,0:T(8,128)(2,1)}) fusion(f32[64,6,2048]{2,1,0:T(8,128)} %reshape.152, f32[64,2048]{1,0:T(8,128)} %convert_element_type.93, pred[64,6]{1,0:T(8,128)(4,1)S(1)} %copy.34, f32[64,6]{1,0:T(8,128)S(1)} %copy.29, f32[64,6,2048]{2,1,0:T(8,128)} %reshape.158), kind=kLoop, calls=%fused_computation.22 | loop fusion | flops 5242496 | bytes 7343488 | tf_op jit(solution)/shard_map/reduce_sum | solution.py:54
  293.8 6.6 %copy.46 = bf16[1,1408,2048]{2,1,0:T(8,128)(2,1)} copy(bf16[1,1408,2048]{2,1,0:T(8,128)(2,1)} %get-tuple-element.36) | data formatting | bytes 11534336
  (68 shorter events, 28.9 us)
Async XLA Ops:
  18.4 7.3 %copy-start.3 = (f32[64,6]{0,1:T(8,128)S(1)}, f32[64,6]{0,1:T(8,128)}, u32[]{:S(2)}) copy-start(f32[64,6]{0,1:T(8,128)} %param.13) | copy-start | bytes 4612
  18.4 7.5 %copy-start.1 = (bf16[64,2048]{1,0:T(8,128)(2,1)S(1)}, bf16[64,2048]{1,0:T(8,128)(2,1)}, u32[]{:S(2)}) copy-start(bf16[64,2048]{1,0:T(8,128)(2,1)} %param.17) | copy-start | bytes 786436
  18.4 55.5 %all-to-all-start = ((bf16[16,32,2048]{2,1,0:T(8,128)(2,1)}), bf16[16,32,2048]{2,1,0:T(8,128)(2,1)}, u32[]{:S(2)}, u32[]{:S(2)}) async-start(bf16[16,32,2048]{2,1,0:T(8,128)(2,1)} %bitcast.69), calls=%async_computation | async-start | bytes 4194304 | tf_op jit(solution)/shard_map/all_to_all | solution.py:85
  73.9 52.5 %all-to-all-start.2 = ((bf16[16,32,2048]{2,1,0:T(8,128)(2,1)}), bf16[16,32,2048]{2,1,0:T(8,128)(2,1)S(1)}, u32[]{:S(2)}, u32[]{:S(2)}) async-start(bf16[16,32,2048]{2,1,0:T(8,128)(2,1)} %bitcast.70), calls=%async_computation.2 | async-start | bytes 4194304 | tf_op jit(solution)/shard_map/all_to_all | solution.py:86
  78.9 214.9 %all-reduce.5.cloned.1.call-start = ((), (), s32[]{:S(2)}) async-start(), calls=%async_computation.4 | async-start | bytes 34603008 | tf_op jit(solution)/shard_map/psum | solution.py:109
  126.4 6.0 %copy-start.4 = (f32[512,1408]{1,0:T(8,128)S(1)}, f32[512,1408]{1,0:T(8,128)}, u32[]{:S(2)}) copy-start(f32[512,1408]{1,0:T(8,128)} %fusion.6) | copy-start | bytes 8650756
  140.3 5.0 %copy-start.8 = (bf16[512,1408]{1,0:T(8,128)(2,1)}, bf16[512,1408]{1,0:T(8,128)(2,1)S(1)}, u32[]{:S(2)}) copy-start(bf16[512,1408]{1,0:T(8,128)(2,1)S(1)} %get-tuple-element.32) | copy-start | bytes 4325380
  140.3 5.0 %copy-start.5 = (bf16[512,1408]{1,0:T(8,128)(2,1)}, bf16[512,1408]{1,0:T(8,128)(2,1)S(1)}, u32[]{:S(2)}) copy-start(bf16[512,1408]{1,0:T(8,128)(2,1)S(1)} %get-tuple-element.30) | copy-start | bytes 4325380
  140.3 12.4 %copy-start.7 = (bf16[512,1408]{1,0:T(8,128)(2,1)}, bf16[512,1408]{1,0:T(8,128)(2,1)S(1)}, u32[]{:S(2)}) copy-start(bf16[512,1408]{1,0:T(8,128)(2,1)S(1)} %get-tuple-element.31) | copy-start | bytes 4325380
  160.0 1.4 copy-start.9
  168.6 52.3 %all-to-all-start.1 = ((bf16[16,32,2048]{2,1,0:T(8,128)(2,1)}), bf16[16,32,2048]{2,1,0:T(8,128)(2,1)S(1)}, u32[]{:S(2)}, u32[]{:S(2)}) async-start(bf16[16,32,2048]{2,1,0:T(8,128)(2,1)} %bitcast.79), calls=%async_computation.1 | async-start | bytes 4194304 | tf_op jit(solution)/shard_map/all_to_all | solution.py:44
  173.3 7.0 %copy-start.6 = (bf16[512,1408]{1,0:T(8,128)(2,1)S(1)}, bf16[512,1408]{1,0:T(8,128)(2,1)}, u32[]{:S(2)}) copy-start(bf16[512,1408]{1,0:T(8,128)(2,1)} %copy-done.5) | copy-start | bytes 4325380
  188.9 37.8 %copy-start.2 = (s32[64,6]{0,1:T(8,128)S(1)}, s32[64,6]{0,1:T(8,128)}, u32[]{:S(2)}) copy-start(s32[64,6]{0,1:T(8,128)} %param.12) | copy-start | bytes 4612
  220.9 52.4 %all-to-all-start.3 = ((bf16[16,32,2048]{2,1,0:T(8,128)(2,1)}), bf16[16,32,2048]{2,1,0:T(8,128)(2,1)}, u32[]{:S(2)}, u32[]{:S(2)}) async-start(bf16[16,32,2048]{2,1,0:T(8,128)(2,1)} %bitcast.76), calls=%async_computation.3 | async-start | bytes 4194304 | tf_op jit(solution)/shard_map/all_to_all | solution.py:44
  293.8 6.6 %copy-start = (bf16[1,1408,2048]{2,1,0:T(8,128)(2,1)S(1)}, bf16[1,1408,2048]{2,1,0:T(8,128)(2,1)}, u32[]{:S(2)}) copy-start(bf16[1,1408,2048]{2,1,0:T(8,128)(2,1)} %get-tuple-element.37) | copy-start | bytes 17301508
  293.8 9.2 %slice-start = ((s8[5767168]{0:T(1024)(128)(4,1)}), s8[4194304]{0:T(1024)(128)(4,1)S(1)}, s32[]{:S(2)}) async-start(s8[5767168]{0:T(1024)(128)(4,1)} %bitcast.71), calls=%async_computation.5 | async-start | bytes 8388608
  300.4 2.7 slice-start.1
Sparse Core Ops, SparseCore 0:
  160.2 60.2 all-reduce.4
where the time goes:
time: 313 us; the launch traced here: 312 us
  waiting for transfers between devices  146 us (47%)
  matrix products  64.6 us (21%)
  local copies, waits for them, and re-layouts  46 us (15%)
  starting transfers between devices  21.9 us (7%)
  other arithmetic  19.7 us (6%)
  between operations  14.3 us (5%)
    all_to_all x2, waiting for transfers between devices, bring_back(): lax.all_to_all(summed.astype(jnp.bfloat16), 'expert', split_axis=0, conca...  66.9 us
    all_to_all x1, waiting for transfers between devices, body(): lax.all_to_all(sent_rows, 'expert', split_axis=0, concat_axis=0, tiled=True)  40.1 us
    all_to_all x1, waiting for transfers between devices, body(): lax.all_to_all(sent_grads, 'expert', split_axis=0, concat_axis=0, tiled=T...  39 us
    dot_general x3, matrix products, contract_cols(): lax.dot_general(left, right, (((1,), (1,)), ((), ())), preferred_element_...  22.2 us
    dot_general x3, matrix products, contract_rows(): lax.dot_general(left, right, (((0,), (0,)), ((), ())), preferred_element_...  19.7 us
    gather x4, local copies, waits for them, and re-layouts, bring_back(): picked = jnp.take(returned, slot_rows, axis=0)  17.5 us
    unnamed x30, local copies, waits for them, and re-layouts  14.8 us
    all_to_all x2, starting transfers between devices, bring_back(): lax.all_to_all(summed.astype(jnp.bfloat16), 'expert', split_axis=0, conca...  9.46 us
  transfers between devices with their start and end apart: 5, of which 4 were waited for; matrix products, arithmetic and copies ran while one was open for 23% of the time, Pallas kernels for 0%

commit v1 on v0

v1 whole, which is shorter than its diff:
```python
import jax
import jax.numpy as jnp
from jax import lax
from jax.sharding import PartitionSpec as P


def contract_rows(left, right):
    return lax.dot_general(
        left, right, (((0,), (0,)), ((), ())), preferred_element_type=jnp.float32
    )


def contract_cols(left, right):
    return lax.dot_general(
        left, right, (((1,), (1,)), ((), ())), preferred_element_type=jnp.float32
    )


def exchange(rows):
    return lax.all_to_all(rows, "expert", split_axis=0, concat_axis=0, tiled=True)


def gather_features(rows):
    if lax.axis_size("tensor") == 1:
        return rows
    return lax.all_gather(rows, "tensor", axis=1, tiled=True)


def scatter_features(rows):
    if lax.axis_size("tensor") == 1:
        return rows
    return lax.psum_scatter(rows, "tensor", scatter_dimension=1, tiled=True)


def add_other_batch(term):
    count = lax.axis_size("dp")
    total = term.astype(jnp.float32)
    moved = term
    for _ in range(count - 1):
        moved = lax.ppermute(moved, "dp", [(i, (i + 1) % count) for i in range(count)])
        total = total + moved.astype(jnp.float32)
    return total.astype(jnp.bfloat16)[None]


def body(tokens, expert_ids, route_weights, w_gate, w_up, w_down, out_grad):
    experts = lax.axis_size("expert")
    tok_rows, choose = expert_ids.shape
    capacity = tok_rows * 8 // experts
    slots = experts * capacity

    named = (expert_ids[:, :, None] == jnp.arange(experts, dtype=jnp.int32)).astype(jnp.float32)
    member = jnp.sum(named, axis=1)
    weight = jnp.sum(named * route_weights[:, :, None], axis=1)
    earlier = (
        jnp.arange(tok_rows)[:, None] > jnp.arange(tok_rows)[None, :]
    ).astype(jnp.bfloat16)
    position = jnp.dot(earlier, member.astype(jnp.bfloat16), preferred_element_type=jnp.float32)
    place = jnp.where(member > 0, position, -1.0)
    hit = place[:, :, None] == jnp.arange(capacity, dtype=jnp.float32)
    select = hit.reshape(tok_rows, slots).astype(jnp.bfloat16)
    spread = jnp.where(hit, weight[:, :, None], 0.0).reshape(tok_rows, slots)
    slot_weight = jnp.sum(spread, axis=0)
    coarse = spread.astype(jnp.bfloat16)
    fine = (spread - coarse.astype(jnp.float32)).astype(jnp.bfloat16)

    full_tokens = gather_features(tokens)
    full_grads = gather_features(out_grad)
    sent_rows = contract_rows(select, full_tokens).astype(jnp.bfloat16)
    expert_rows = exchange(sent_rows)
    sent_grads = (slot_weight[:, None] * contract_rows(select, full_grads)).astype(jnp.bfloat16)
    expert_rows, sent_grads = lax.optimization_barrier((expert_rows, sent_grads))
    expert_grads = exchange(sent_grads)

    gate_matrix = w_gate[0]
    up_matrix = w_up[0]
    down_matrix = w_down[0]
    gate_value = contract_cols(expert_rows, gate_matrix)
    up_value = contract_cols(expert_rows, up_matrix)
    sigma = jax.nn.sigmoid(gate_value)
    silu = gate_value * sigma
    hidden = (silu * up_value).astype(jnp.bfloat16)
    part = jnp.dot(hidden, down_matrix, preferred_element_type=jnp.float32).astype(jnp.bfloat16)
    part, expert_grads = lax.optimization_barrier((part, expert_grads))
    returned = exchange(scatter_features(part))

    grad_hidden = contract_cols(expert_grads, down_matrix)
    gate_rows = (grad_hidden * up_value * sigma * (1.0 + gate_value * (1.0 - sigma))).astype(
        jnp.bfloat16
    )
    up_rows = (grad_hidden * silu).astype(jnp.bfloat16)
    down_term = contract_rows(hidden, expert_grads).astype(jnp.bfloat16)
    gate_term = contract_rows(gate_rows, expert_rows).astype(jnp.bfloat16)
    up_term = contract_rows(up_rows, expert_rows).astype(jnp.bfloat16)
    gate_rows, up_rows, down_term, gate_term, up_term = lax.optimization_barrier(
        (gate_rows, up_rows, down_term, gate_term, up_term)
    )
    down_out = add_other_batch(down_term)
    gate_out = add_other_batch(gate_term)
    up_out = add_other_batch(up_term)
    grad_part = (
        jnp.dot(gate_rows, gate_matrix, preferred_element_type=jnp.float32)
        + jnp.dot(up_rows, up_matrix, preferred_element_type=jnp.float32)
    ).astype(jnp.bfloat16)
    grad_part, returned = lax.optimization_barrier((grad_part, returned))
    returned_grads = exchange(scatter_features(grad_part))

    layer_out = (
        jnp.dot(coarse, returned, preferred_element_type=jnp.float32)
        + jnp.dot(fine, returned, preferred_element_type=jnp.float32)
    ).astype(jnp.bfloat16)
    products = contract_cols(out_grad, returned).reshape(tok_rows, experts, capacity)
    dots = jnp.sum(jnp.where(hit, products, 0.0), axis=2)
    weight_dots = jnp.sum(named * dots[:, None, :], axis=2)
    if lax.axis_size("tensor") > 1:
        weight_dots = lax.psum(weight_dots, "tensor")
    grad_tokens = jnp.dot(select, returned_grads, preferred_element_type=jnp.float32).astype(
        jnp.bfloat16
    )
    return (layer_out, grad_tokens, weight_dots, gate_out, up_out, down_out)


def solution(mesh):
    placed = (
        P(("dp", "expert"), "tensor"),
        P(("dp", "expert"), None),
        P(("dp", "expert"), None),
        P("expert", "tensor", None),
        P("expert", "tensor", None),
        P("expert", "tensor", None),
        P(("dp", "expert"), "tensor"),
    )
    return jax.shard_map(
        body,
        mesh=mesh,
        in_specs=placed,
        out_specs=(
            P(("dp", "expert"), "tensor"),
            P(("dp", "expert"), "tensor"),
            P(("dp", "expert"), None),
            P("expert", "tensor", None),
            P("expert", "tensor", None),
            P("expert", "tensor", None),
        ),
        check_vma=False,
    )
```

time: 313 us -> 248 us (0.79)
  local copies, waits for them, and re-layouts: 46 us -> 1.56 us
  waiting for transfers between devices: 146 us -> 126 us
  between operations: 14.3 us -> 0.86 us
  other arithmetic: 19.7 us -> 30.6 us
    broadcast_in_dim x0 -> x3, other arithmetic: none -> 28.6 us  [add_other_batch(): return total.astype(jnp.bfloat16)[None]]
    gather x7 -> x0, local copies, waits for them, and re-layouts: 25.9 us -> none  [the longest x4 17.5 us: bring_back(): picked = jnp.take(returned, slot_rows, axis=0)]
    all_to_all x4, waiting for transfers between devices: 146 us -> 126 us  [exchange(): lax.all_to_all(rows, 'expert', split_axis=0, concat_axis=0, tiled=True)]
    unnamed x30, local copies, waits for them, and re-layouts: 14.8 us -> 1.27 us
    convert_element_type x5 -> x2, other arithmetic: 9.49 us -> 0.27 us  [the longest x1 0.13 us: body(): fine = (spread - coarse.astype(jnp.float32)).astype(jnp.bfloat16)]
    reduce_sum x2 -> x4, other arithmetic: 6.98 us -> 1.54 us  [the longest x1 0.72 us: body(): member = jnp.sum(named, axis=1)]
    dot_general x0 -> x4, matrix products: none -> 4.66 us  [the longest x1 2.82 us: body(): jnp.dot(select, returned_grads, preferred_element_type=jnp.float32)]
    dot_general x1, matrix products: 8.52 us -> 4.62 us  [body(): jnp.dot(gate_rows, gate_matrix, preferred_element_type=jnp.float32)]
  transfers between devices with their start and end apart: 5 -> 7, of which waited for: 4 -> 4; matrix products, arithmetic and copies ran while one was open for 23% -> 26% of each run, Pallas kernels for 0% -> 0%
where the time goes in v1:
time: 248 us
  waiting for transfers between devices  126 us (51%)
  matrix products  65.9 us (27%)
  other arithmetic  30.6 us (12%)
  starting transfers between devices  23.2 us (9%)
    all_to_all x4, waiting for transfers between devices, exchange(): lax.all_to_all(rows, 'expert', split_axis=0, concat_axis=0, tiled=True)  126 us
    broadcast_in_dim x3, other arithmetic, add_other_batch(): return total.astype(jnp.bfloat16)[None]  28.6 us
    dot_general x4, matrix products, contract_cols(): lax.dot_general(left, right, (((1,), (1,)), ((), ())), preferred_element_...  23 us
    dot_general x5, matrix products, contract_rows(): lax.dot_general(left, right, (((0,), (0,)), ((), ())), preferred_element_...  22.8 us
    all_to_all x4, starting transfers between devices, exchange(): lax.all_to_all(rows, 'expert', split_axis=0, concat_axis=0, tiled=True)  22.6 us
    dot_general x1, matrix products, body(): jnp.dot(up_rows, up_matrix, preferred_element_type=jnp.float32)  6.21 us
  transfers between devices with their start and end apart: 7, of which 4 were waited for; matrix products, arithmetic and copies ran while one was open for 26% of the time, Pallas kernels for 0%

profile of v1, /device:TPU:12, one launch (start us, length us, event | category | flops | bytes accessed | tf_op | source)
XLA Modules:
  0.0 247.7 jit_solution(2042360573128443163)
XLA Ops:
  1.7 3.0 %convolution_convert_fusion.3 = bf16[512,2048]{1,0:T(8,128)(2,1)} fusion(pred[64,512]{0,1:T(32,128)(4,1)S(1)} %bitcast_compare_fusion, bf16[64,2048]{1,0:T(8,128)(2,1)} %param.7), kind=kOutput, calls=%fused_computation.23 | convolution fusion | flops 135266304 | bytes 2392064 | tf_op jit(solution)/shard_map/dot_general | solution.py:8
  4.7 7.2 %all-to-all-start = ((bf16[16,32,2048]{2,1,0:T(8,128)(2,1)}), bf16[16,32,2048]{2,1,0:T(8,128)(2,1)S(1)}, u32[]{:S(2)}, u32[]{:S(2)}) async-start(bf16[16,32,2048]{2,1,0:T(8,128)(2,1)} %bitcast.2), calls=%async_computation | async-start | bytes 4194304 | tf_op jit(solution)/shard_map/all_to_all | solution.py:20
  12.1 2.0 multiply_convert_fusion
  14.1 45.9 %all-to-all-done = bf16[16,32,2048]{2,1,0:T(8,128)(2,1)S(1)} async-done(((bf16[16,32,2048]{2,1,0:T(8,128)(2,1)}), bf16[16,32,2048]{2,1,0:T(8,128)(2,1)S(1)}, u32[]{:S(2)}, u32[]{:S(2)}) %all-to-all-start) | async-done | bytes 2097184 | tf_op jit(solution)/shard_map/all_to_all | solution.py:20
  60.0 4.9 %all-to-all-start.1 = ((bf16[16,32,2048]{2,1,0:T(8,128)(2,1)}), bf16[16,32,2048]{2,1,0:T(8,128)(2,1)}, u32[]{:S(2)}, u32[]{:S(2)}) async-start(bf16[16,32,2048]{2,1,0:T(8,128)(2,1)} %bitcast.7), calls=%async_computation.1 | async-start | bytes 4194304 | tf_op jit(solution)/shard_map/all_to_all | solution.py:20
  64.9 6.0 %fusion.13 = f32[512,1408]{1,0:T(8,128)S(1)} fusion(bf16[512,2048]{1,0:T(8,128)(2,1)S(1)} %bitcast.91, bf16[1,1408,2048]{2,1,0:T(8,128)(2,1)} %param.10), kind=kOutput, calls=%fused_computation.19 | convolution fusion | flops 2952790016 | bytes 10747904 | tf_op jit(solution)/shard_map/dot_general | solution.py:14
  70.9 8.9 %multiply_convert_fusion.3 = (bf16[512,1408]{1,0:T(8,128)(2,1)S(1)}, f32[512,1408]{1,0:T(8,128)}) fusion(f32[512,1408]{1,0:T(8,128)S(1)} %fusion.13, bf16[512,2048]{1,0:T(8,128)(2,1)S(1)} %bitcast.92, bf16[1,1408,2048]{2,1,0:T(8,128)(2,1)} %param.11), kind=kOutput, calls=%fused_computation.27 | convolution fusion | flops 2957115392 | bytes 15073280 | tf_op jit(solution)/shard_map/dot_general | solution.py:14
  81.0 4.6 %fusion.17 = bf16[512,2048]{1,0:T(8,128)(2,1)} fusion(bf16[512,1408]{1,0:T(8,128)(2,1)S(1)} %get-tuple-element.32, bf16[1,1408,2048]{2,1,0:T(8,128)(2,1)S(1)} %bitcast.97), kind=kOutput, calls=%fused_computation.24 | convolution fusion | flops 2953838592 | bytes 9306112 | tf_op jit(solution)/shard_map/dot_general | solution.py:82
  85.6 27.0 %all-to-all-done.1 = bf16[16,32,2048]{2,1,0:T(8,128)(2,1)} async-done(((bf16[16,32,2048]{2,1,0:T(8,128)(2,1)}), bf16[16,32,2048]{2,1,0:T(8,128)(2,1)}, u32[]{:S(2)}, u32[]{:S(2)}) %all-to-all-start.1) | async-done | bytes 2097184 | tf_op jit(solution)/shard_map/all_to_all | solution.py:20
  112.6 7.9 %convolution_convert_fusion.2 = bf16[1408,2048]{1,0:T(8,128)(2,1)} fusion(bf16[512,1408]{1,0:T(8,128)(2,1)} %copy-done.7, bf16[512,2048]{1,0:T(8,128)(2,1)} %bitcast.8), kind=kOutput, calls=%fused_computation.5 | convolution fusion | flops 2955673600 | bytes 9306112 | tf_op jit(solution)/shard_map/dot_general | solution.py:8
  120.4 7.4 %multiply_convert_fusion.1 = (bf16[512,1408]{1,0:T(8,128)(2,1)S(1)}, bf16[512,1408]{1,0:T(8,128)(2,1)S(1)}) fusion(f32[512,1408]{1,0:T(8,128)S(1)} %copy-done.3, f32[512,1408]{1,0:T(8,128)S(1)} %copy-done.8, bf16[512,2048]{1,0:T(8,128)(2,1)} %bitcast.8, bf16[1,1408,2048]{2,1,0:T(8,128)(2,1)} %param.12), kind=kOutput, calls=%fused_computation.25 | convolution fusion | flops 2962161664 | bytes 16515072 | tf_op jit(solution)/shard_map/dot_general | solution.py:14
  127.9 5.0 %convolution_convert_fusion = bf16[1408,2048]{1,0:T(8,128)(2,1)} fusion(bf16[512,1408]{1,0:T(8,128)(2,1)S(1)} %get-tuple-element.21, bf16[512,2048]{1,0:T(8,128)(2,1)S(1)} %bitcast.93), kind=kOutput, calls=%fused_computation.3 | convolution fusion | flops 2955673600 | bytes 9306112 | tf_op jit(solution)/shard_map/dot_general | solution.py:8
  132.9 5.0 %convolution_convert_fusion.1 = bf16[1408,2048]{1,0:T(8,128)(2,1)} fusion(bf16[512,1408]{1,0:T(8,128)(2,1)S(1)} %get-tuple-element.20, bf16[512,2048]{1,0:T(8,128)(2,1)S(1)} %bitcast.94), kind=kOutput, calls=%fused_computation.4 | convolution fusion | flops 2955673600 | bytes 9306112 | tf_op jit(solution)/shard_map/dot_general | solution.py:8
  137.8 4.7 %all-to-all-start.2 = ((bf16[16,32,2048]{2,1,0:T(8,128)(2,1)}), bf16[16,32,2048]{2,1,0:T(8,128)(2,1)S(1)}, u32[]{:S(2)}, u32[]{:S(2)}) async-start(bf16[16,32,2048]{2,1,0:T(8,128)(2,1)} %bitcast.90), calls=%async_computation.2 | async-start | bytes 4194304 | tf_op jit(solution)/shard_map/all_to_all | solution.py:20
  143.5 6.2 %fusion.7 = f32[512,2048]{1,0:T(8,128)S(1)} fusion(bf16[512,1408]{1,0:T(8,128)(2,1)} %copy-done.6, bf16[1,1408,2048]{2,1,0:T(8,128)(2,1)} %param.11), kind=kOutput, calls=%fused_computation.13 | convolution fusion | flops 2952790016 | bytes 11403264 | tf_op jit(solution)/shard_map/dot_general | solution.py:102
  149.7 4.6 %add_convert_fusion.3 = bf16[512,2048]{1,0:T(8,128)(2,1)} fusion(f32[512,2048]{1,0:T(8,128)S(1)} %fusion.7, bf16[512,1408]{1,0:T(8,128)(2,1)S(1)} %copy-done.5, bf16[1,1408,2048]{2,1,0:T(8,128)(2,1)S(1)} %bitcast.99), kind=kOutput, calls=%fused_computation.21 | convolution fusion | flops 2954887168 | bytes 13500416 | tf_op jit(solution)/shard_map/dot_general | solution.py:101
  154.3 36.7 %all-to-all-done.2 = bf16[16,32,2048]{2,1,0:T(8,128)(2,1)S(1)} async-done(((bf16[16,32,2048]{2,1,0:T(8,128)(2,1)}), bf16[16,32,2048]{2,1,0:T(8,128)(2,1)S(1)}, u32[]{:S(2)}, u32[]{:S(2)}) %all-to-all-start.2) | async-done | bytes 2097184 | tf_op jit(solution)/shard_map/all_to_all | solution.py:20
  191.1 5.8 %all-to-all-start.3 = ((bf16[16,32,2048]{2,1,0:T(8,128)(2,1)}), bf16[16,32,2048]{2,1,0:T(8,128)(2,1)}, u32[]{:S(2)}, u32[]{:S(2)}) async-start(bf16[16,32,2048]{2,1,0:T(8,128)(2,1)} %bitcast.95), calls=%async_computation.3 | async-start | bytes 4194304 | tf_op jit(solution)/shard_map/all_to_all | solution.py:20
  199.0 1.2 fusion.22
  200.2 10.4 %fusion = bf16[1,1408,2048]{2,1,0:T(8,128)(2,1)} fusion(bf16[1408,2048]{1,0:T(8,128)(2,1)} %collective-permute-done, bf16[1408,2048]{1,0:T(8,128)(2,1)} %convolution_convert_fusion.1), kind=kLoop, calls=%fused_computation.6 | loop fusion | flops 11534336 | bytes 17301504 | tf_op jit(solution)/shard_map/broadcast_in_dim | solution.py:42
  210.5 10.3 %fusion.1 = bf16[1,1408,2048]{2,1,0:T(8,128)(2,1)} fusion(bf16[1408,2048]{1,0:T(8,128)(2,1)} %collective-permute-done.1, bf16[1408,2048]{1,0:T(8,128)(2,1)} %convolution_convert_fusion), kind=kLoop, calls=%fused_computation.7 | loop fusion | flops 11534336 | bytes 17301504 | tf_op jit(solution)/shard_map/broadcast_in_dim | solution.py:42
  220.9 7.9 %fusion.2 = bf16[1,1408,2048]{2,1,0:T(8,128)(2,1)} fusion(bf16[1408,2048]{1,0:T(8,128)(2,1)} %collective-permute-done.2, bf16[1408,2048]{1,0:T(8,128)(2,1)S(1)} %bitcast.89), kind=kLoop, calls=%fused_computation.8 | loop fusion | flops 11534336 | bytes 17301504 | tf_op jit(solution)/shard_map/broadcast_in_dim | solution.py:42
  228.8 16.1 %all-to-all-done.3 = bf16[16,32,2048]{2,1,0:T(8,128)(2,1)} async-done(((bf16[16,32,2048]{2,1,0:T(8,128)(2,1)}), bf16[16,32,2048]{2,1,0:T(8,128)(2,1)}, u32[]{:S(2)}, u32[]{:S(2)}) %all-to-all-start.3) | async-done | bytes 2097184 | tf_op jit(solution)/shard_map/all_to_all | solution.py:20
  244.9 2.8 %fusion.21 = bf16[64,2048]{1,0:T(8,128)(2,1)} fusion(bf16[16,32,2048]{2,1,0:T(8,128)(2,1)} %all-to-all-done.3, f32[64,16]{0,1:T(8,128)S(1)} %convolution_select_fusion), kind=kOutput, calls=%fused_computation.32 | convolution fusion | flops 134381568 | bytes 2363392 | tf_op jit(solution)/shard_map/dot_general | solution.py:116
  (53 shorter events, 5.5 us)
Async XLA Ops:
  0.6 11.5 %copy-start = (bf16[64,2048]{1,0:T(8,128)(2,1)S(1)}, bf16[64,2048]{1,0:T(8,128)(2,1)}, u32[]{:S(2)}) copy-start(bf16[64,2048]{1,0:T(8,128)(2,1)} %param.13) | copy-start | bytes 786436
  4.7 55.3 %all-to-all-start = ((bf16[16,32,2048]{2,1,0:T(8,128)(2,1)}), bf16[16,32,2048]{2,1,0:T(8,128)(2,1)S(1)}, u32[]{:S(2)}, u32[]{:S(2)}) async-start(bf16[16,32,2048]{2,1,0:T(8,128)(2,1)} %bitcast.2), calls=%async_computation | async-start | bytes 4194304 | tf_op jit(solution)/shard_map/all_to_all | solution.py:20
  60.0 52.6 %all-to-all-start.1 = ((bf16[16,32,2048]{2,1,0:T(8,128)(2,1)}), bf16[16,32,2048]{2,1,0:T(8,128)(2,1)}, u32[]{:S(2)}, u32[]{:S(2)}) async-start(bf16[16,32,2048]{2,1,0:T(8,128)(2,1)} %bitcast.7), calls=%async_computation.1 | async-start | bytes 4194304 | tf_op jit(solution)/shard_map/all_to_all | solution.py:20
  64.9 16.1 %slice-start.2 = ((s8[5767168]{0:T(1024)(128)(4,1)}), s8[4194304]{0:T(1024)(128)(4,1)S(1)}, s32[]{:S(2)}) async-start(s8[5767168]{0:T(1024)(128)(4,1)} %bitcast.96), calls=%async_computation.6 | async-start | bytes 8388608
  70.9 8.9 %copy-start.2 = (f32[512,1408]{1,0:T(8,128)}, f32[512,1408]{1,0:T(8,128)S(1)}, u32[]{:S(2)}) copy-start(f32[512,1408]{1,0:T(8,128)S(1)} %fusion.13) | copy-start | bytes 8650756
  70.9 10.1 %slice-start.3 = ((s8[5767168]{0:T(1024)(128)(4,1)}), s8[1572864]{0:T(1024)(128)(4,1)S(1)}, s32[]{:S(2)}) async-start(s8[5767168]{0:T(1024)(128)(4,1)} %bitcast.96), calls=%async_computation.7 | async-start | bytes 3145728
  79.8 1.2 copy-start.7
  112.6 7.9 %copy-start.3 = (f32[512,1408]{1,0:T(8,128)S(1)}, f32[512,1408]{1,0:T(8,128)}, u32[]{:S(2)}) copy-start(f32[512,1408]{1,0:T(8,128)} %copy-done.2) | copy-start | bytes 8650756
  112.6 7.9 %copy-start.8 = (f32[512,1408]{1,0:T(8,128)S(1)}, f32[512,1408]{1,0:T(8,128)}, u32[]{:S(2)}) copy-start(f32[512,1408]{1,0:T(8,128)} %get-tuple-element.33) | copy-start | bytes 8650756
  127.9 5.0 %copy-start.6 = (bf16[512,1408]{1,0:T(8,128)(2,1)}, bf16[512,1408]{1,0:T(8,128)(2,1)S(1)}, u32[]{:S(2)}) copy-start(bf16[512,1408]{1,0:T(8,128)(2,1)S(1)} %get-tuple-element.21) | copy-start | bytes 4325380
  127.9 5.0 %copy-start.4 = (bf16[512,1408]{1,0:T(8,128)(2,1)}, bf16[512,1408]{1,0:T(8,128)(2,1)S(1)}, u32[]{:S(2)}) copy-start(bf16[512,1408]{1,0:T(8,128)(2,1)S(1)} %get-tuple-element.20) | copy-start | bytes 4325380
  137.8 62.3 %collective-permute-start = (bf16[1408,2048]{1,0:T(8,128)(2,1)}, bf16[1408,2048]{1,0:T(8,128)(2,1)}, u32[]{:S(2)}, u32[]{:S(2)}) collective-permute-start(bf16[1408,2048]{1,0:T(8,128)(2,1)} %convolution_convert_fusion.1), channel_id=1, source_target_pairs={{0,16},{16,0},{1,17},{17,1},{2,18},{18,2},{3,19},{19,3},{4,20},{20... | collective-permute-start | bytes 17301512 | tf_op jit(solution)/shard_map/ppermute | solution.py:40
  137.8 53.2 %all-to-all-start.2 = ((bf16[16,32,2048]{2,1,0:T(8,128)(2,1)}), bf16[16,32,2048]{2,1,0:T(8,128)(2,1)S(1)}, u32[]{:S(2)}, u32[]{:S(2)}) async-start(bf16[16,32,2048]{2,1,0:T(8,128)(2,1)} %bitcast.90), calls=%async_computation.2 | async-start | bytes 4194304 | tf_op jit(solution)/shard_map/all_to_all | solution.py:20
  142.6 68.0 %collective-permute-start.1 = (bf16[1408,2048]{1,0:T(8,128)(2,1)}, bf16[1408,2048]{1,0:T(8,128)(2,1)}, u32[]{:S(2)}, u32[]{:S(2)}) collective-permute-start(bf16[1408,2048]{1,0:T(8,128)(2,1)} %convolution_convert_fusion), channel_id=1, source_target_pairs={{0,16},{16,0},{1,17},{17,1},{2,18},{18,2},{3,19},{19,3},{4,20},{20... | collective-permute-start | bytes 17301512 | tf_op jit(solution)/shard_map/ppermute | solution.py:40
  142.7 7.0 %slice-start.4 = ((s8[5767168]{0:T(1024)(128)(4,1)}), s8[4194304]{0:T(1024)(128)(4,1)S(1)}, s32[]{:S(2)}) async-start(s8[5767168]{0:T(1024)(128)(4,1)} %bitcast.98), calls=%async_computation.8 | async-start | bytes 8388608
  142.9 6.8 %slice-start.5 = ((s8[5767168]{0:T(1024)(128)(4,1)}), s8[1572864]{0:T(1024)(128)(4,1)S(1)}, s32[]{:S(2)}) async-start(s8[5767168]{0:T(1024)(128)(4,1)} %bitcast.98), calls=%async_computation.9 | async-start | bytes 3145728
  142.9 6.8 %copy-start.5 = (bf16[512,1408]{1,0:T(8,128)(2,1)S(1)}, bf16[512,1408]{1,0:T(8,128)(2,1)}, u32[]{:S(2)}) copy-start(bf16[512,1408]{1,0:T(8,128)(2,1)} %copy-done.4) | copy-start | bytes 4325380
  142.9 78.0 %collective-permute-start.2 = (bf16[1408,2048]{1,0:T(8,128)(2,1)}, bf16[1408,2048]{1,0:T(8,128)(2,1)}, u32[]{:S(2)}, u32[]{:S(2)}) collective-permute-start(bf16[1408,2048]{1,0:T(8,128)(2,1)} %convolution_convert_fusion.2), channel_id=1, source_target_pairs={{0,16},{16,0},{1,17},{17,1},{2,18},{18,2},{3,19},{19,3},{4,20},{20... | collective-permute-start | bytes 17301512 | tf_op jit(solution)/shard_map/ppermute | solution.py:40
  191.1 6.8 %copy-start.1 = (s32[64,6]{0,1:T(8,128)S(1)}, s32[64,6]{0,1:T(8,128)}, u32[]{:S(2)}) copy-start(s32[64,6]{0,1:T(8,128)} %param.8) | copy-start | bytes 4612
  191.1 53.8 %all-to-all-start.3 = ((bf16[16,32,2048]{2,1,0:T(8,128)(2,1)}), bf16[16,32,2048]{2,1,0:T(8,128)(2,1)}, u32[]{:S(2)}, u32[]{:S(2)}) async-start(bf16[16,32,2048]{2,1,0:T(8,128)(2,1)} %bitcast.95), calls=%async_computation.3 | async-start | bytes 4194304 | tf_op jit(solution)/shard_map/all_to_all | solution.py:20
  200.2 20.7 %slice-start = ((s8[5767168]{0:T(1024)(128)(4,1)}), s8[4194304]{0:T(1024)(128)(4,1)S(1)}, s32[]{:S(2)}) async-start(s8[5767168]{0:T(1024)(128)(4,1)} %bitcast.88), calls=%async_computation.4 | async-start | bytes 8388608
  210.5 10.3 %slice-start.1 = ((s8[5767168]{0:T(1024)(128)(4,1)}), s8[1572864]{0:T(1024)(128)(4,1)S(1)}, s32[]{:S(2)}) async-start(s8[5767168]{0:T(1024)(128)(4,1)} %bitcast.88), calls=%async_computation.5 | async-start | bytes 3145728

commit v2 on v1

--- a/solution.py
+++ b/solution.py
@@ -1,6 +1,9 @@
+import functools
 import jax
 import jax.numpy as jnp
 from jax import lax
+from jax.experimental import pallas as pl
+from jax.experimental.pallas import tpu as pltpu
 from jax.sharding import PartitionSpec as P
 
 
@@ -40,6 +43,124 @@
         moved = lax.ppermute(moved, "dp", [(i, (i + 1) % count) for i in range(count)])
         total = total + moved.astype(jnp.float32)
     return total.astype(jnp.bfloat16)[None]
+
+
+def dispatch_kernel(outer, inner, capacity, x_ref, g_ref, p_ref, rows_ref, grads_ref,
+                    far_x, far_g, far_p, own_x, own_g, far_send, far_recv, near_send, near_recv):
+    me = lax.axis_index("expert")
+    plane, spot = me // inner, me % inner
+
+    def far_id(step):
+        return {"expert": ((plane + step) % outer) * inner + spot}
+
+    def near_id(step):
+        return {"expert": plane * inner + (spot + step) % inner}
+
+    barrier = pltpu.get_barrier_semaphore()
+    for step in range(1, outer):
+        pl.semaphore_signal(barrier, inc=1, device_id=far_id(step), device_id_type=pl.DeviceIdType.MESH)
+    for step in range(1, inner):
+        pl.semaphore_signal(barrier, inc=1, device_id=near_id(step), device_id_type=pl.DeviceIdType.MESH)
+    pl.semaphore_wait(barrier, outer + inner - 2)
+
+    def far_copy(step, kind):
+        source = (x_ref, p_ref.at[(plane + step) % outer], g_ref)[kind]
+        landing = (far_x, far_p, far_g)[kind]
+        return pltpu.make_async_remote_copy(
+            src_ref=source,
+            dst_ref=landing.at[step - 1],
+            send_sem=far_send.at[step - 1, kind],
+            recv_sem=far_recv.at[step - 1, kind],
+            device_id=far_id(step),
+            device_id_type=pl.DeviceIdType.MESH,
+        )
+
+    def near_copy(block, step, kind):
+        source = (own_x, own_g)[kind]
+        landing = (rows_ref, grads_ref)[kind]
+        start = pl.multiple_of(((spot + step) % inner) * capacity, capacity)
+        origin = (plane + outer - block) % outer
+        place = pl.multiple_of((origin * inner + spot) * capacity, capacity)
+        return pltpu.make_async_remote_copy(
+            src_ref=source.at[block, pl.ds(start, capacity)],
+            dst_ref=landing.at[pl.ds(place, capacity)],
+            send_sem=near_send.at[block, step - 1, kind],
+            recv_sem=near_recv.at[block, step - 1, kind],
+            device_id=near_id(step),
+            device_id_type=pl.DeviceIdType.MESH,
+        )
+
+    for kind in range(3):
+        for step in range(1, outer):
+            far_copy(step, kind).start()
+
+    def choose(block, kind):
+        if block == 0:
+            picks = p_ref[plane]
+            values = (x_ref, g_ref)[kind][...]
+        else:
+            if kind == 0:
+                far_copy(block, 0).wait_recv()
+                far_copy(block, 1).wait_recv()
+            else:
+                far_copy(block, 2).wait_recv()
+            picks = far_p[block - 1]
+            values = (far_x, far_g)[kind][block - 1]
+        if kind == 0:
+            lane = lax.broadcasted_iota(jnp.int32, picks.shape, 1)
+            taken = (picks.astype(jnp.float32) > 0.0) & (lane < values.shape[0])
+            picks = jnp.where(taken, 1.0, 0.0).astype(jnp.bfloat16)
+        twice = jnp.concatenate([values, values], axis=0)
+        chosen = jnp.dot(picks, twice, preferred_element_type=jnp.float32).astype(jnp.bfloat16)
+        kept = (own_x, own_g)[kind]
+        kept[block] = chosen
+        for step in range(1, inner):
+            near_copy(block, step, kind).start()
+        origin = (plane + outer - block) % outer
+        place = pl.multiple_of((origin * inner + spot) * capacity, capacity)
+        start = pl.multiple_of(spot * capacity, capacity)
+        landing = (rows_ref, grads_ref)[kind]
+        landing[pl.ds(place, capacity)] = kept[block, pl.ds(start, capacity)]
+
+    choose(0, 0)
+    choose(0, 1)
+    for kind in range(2):
+        for block in range(1, outer):
+            choose(block, kind)
+    for kind in range(3):
+        for step in range(1, outer):
+            far_copy(step, kind).wait_send()
+    for kind in range(2):
+        for block in range(outer):
+            for step in range(1, inner):
+                near_copy(block, step, kind).wait()
+
+
+def dispatch(tokens, grads, picks, outer, inner, capacity):
+    rows, width = tokens.shape
+    slots = outer * inner * capacity
+    bf16 = jnp.bfloat16
+    landed = jax.ShapeDtypeStruct((slots, width), bf16)
+    return pl.pallas_call(
+        functools.partial(dispatch_kernel, outer, inner, capacity),
+        out_shape=(landed, landed),
+        in_specs=[pl.BlockSpec(memory_space=pltpu.VMEM)] * 3,
+        out_specs=[pl.BlockSpec(memory_space=pltpu.VMEM)] * 2,
+        scratch_shapes=[
+            pltpu.VMEM((outer - 1, rows, width), bf16),
+            pltpu.VMEM((outer - 1, rows, width), bf16),
+            pltpu.VMEM((outer - 1, inner * capacity, 2 * rows), bf16),
+            pltpu.VMEM((outer, inner * capacity, width), bf16),
+            pltpu.VMEM((outer, inner * capacity, width), bf16),
+            pltpu.SemaphoreType.DMA((outer - 1, 3)),
+            pltpu.SemaphoreType.DMA((outer - 1, 3)),
+            pltpu.SemaphoreType.DMA((outer, inner - 1, 2)),
+            pltpu.SemaphoreType.DMA((outer, inner - 1, 2)),
+        ],
+        compiler_params=pltpu.CompilerParams(
+            collective_id=0, has_side_effects=True, vmem_limit_bytes=32 * 1024 * 1024
+        ),
+    )(tokens, grads, picks)
 
 
 def body(tokens, expert_ids, route_weights, w_gate, w_up, w_down, out_grad):
@@ -59,17 +180,15 @@
     hit = place[:, :, None] == jnp.arange(capacity, dtype=jnp.float32)
     select = hit.reshape(tok_rows, slots).astype(jnp.bfloat16)
     spread = jnp.where(hit, weight[:, :, None], 0.0).reshape(tok_rows, slots)
-    slot_weight = jnp.sum(spread, axis=0)
     coarse = spread.astype(jnp.bfloat16)
     fine = (spread - coarse.astype(jnp.float32)).astype(jnp.bfloat16)
 
     full_tokens = gather_features(tokens)
     full_grads = gather_features(out_grad)
-    sent_rows = contract_rows(select, full_tokens).astype(jnp.bfloat16)
-    expert_rows = exchange(sent_rows)
-    sent_grads = (slot_weight[:, None] * contract_rows(select, full_grads)).astype(jnp.bfloat16)
-    expert_rows, sent_grads = lax.optimization_barrier((expert_rows, sent_grads))
-    expert_grads = exchange(sent_grads)
+    inner = 4
+    outer = experts // inner
+    picks = jnp.concatenate([coarse, fine], axis=0).T.reshape(outer, inner * capacity, 2 * tok_rows)
+    expert_rows, expert_grads = dispatch(full_tokens, full_grads, picks, outer, inner, capacity)
 
     gate_matrix = w_gate[0]
     up_matrix = w_up[0]
@@ -91,8 +210,8 @@
     down_term = contract_rows(hidden, expert_grads).astype(jnp.bfloat16)
     gate_term = contract_rows(gate_rows, expert_rows).astype(jnp.bfloat16)
     up_term = contract_rows(up_rows, expert_rows).astype(jnp.bfloat16)
-    gate_rows, up_rows, down_term, gate_term, up_term = lax.optimization_barrier(
-        (gate_rows, up_rows, down_term, gate_term, up_term)
+    gate_rows, up_rows, down_term, gate_term, up_term, returned = lax.optimization_barrier(
+        (gate_rows, up_rows, down_term, gate_term, up_term, returned)
     )
     down_out = add_other_batch(down_term)
     gate_out = add_other_batch(gate_term)
@@ -101,7 +220,6 @@
         jnp.dot(gate_rows, gate_matrix, preferred_element_type=jnp.float32)
         + jnp.dot(up_rows, up_matrix, preferred_element_type=jnp.float32)
     ).astype(jnp.bfloat16)
-    grad_part, returned = lax.optimization_barrier((grad_part, returned))
     returned_grads = exchange(scatter_features(grad_part))
 
     layer_out = (
@@ -113,6 +231,9 @@
     weight_dots = jnp.sum(named * dots[:, None, :], axis=2)
     if lax.axis_size("tensor") > 1:
         weight_dots = lax.psum(weight_dots, "tensor")
+    returned_grads, gate_out, up_out, down_out = lax.optimization_barrier(
+        (returned_grads, gate_out, up_out, down_out)
+    )
     grad_tokens = jnp.dot(select, returned_grads, preferred_element_type=jnp.float32).astype(
         jnp.bfloat16
     )

time: 248 us -> 215 us (0.87)
  waiting for transfers between devices: 126 us -> 37 us
  Pallas kernels: 0 us -> 66 us
  starting transfers between devices: 23.2 us -> 15.8 us
  matrix products: 65.9 us -> 60 us
    all_to_all x4 -> x2, waiting for transfers between devices: 126 us -> 37 us  [exchange(): lax.all_to_all(rows, 'expert', split_axis=0, concat_axis=0, tiled=True)]
    pallas_call x0 -> x1, Pallas kernels: none -> 66 us  [dispatch(): pl.pallas_call(functools.partial(dispatch_kernel, outer, inner, capacity)...]
    all_to_all x4 -> x2, starting transfers between devices: 22.6 us -> 15.2 us  [exchange(): lax.all_to_all(rows, 'expert', split_axis=0, concat_axis=0, tiled=True)]
    dot_general x5 -> x3, matrix products: 22.8 us -> 17.8 us  [contract_rows(): lax.dot_general(left, right, (((0,), (0,)), ((), ())), preferred_element_...]
    dot_general x4, matrix products: 23 us -> 20.4 us  [contract_cols(): lax.dot_general(left, right, (((1,), (1,)), ((), ())), preferred_element_...]
  transfers between devices with their start and end apart: 7 -> 5, of which waited for: 4 -> 2; matrix products, arithmetic and copies ran while one was open for 26% -> 34% of each run, Pallas kernels for 0% -> 0%
where the time goes in v2:
time: 215 us; the launch traced here: 214 us
  Pallas kernels  66 us (31%)
  matrix products  60 us (28%)
  waiting for transfers between devices  37 us (17%)
  other arithmetic  30.5 us (14%)
  starting transfers between devices  15.8 us (7%)
  local copies, waits for them, and re-layouts  3.53 us (2%)
    pallas_call x1, Pallas kernels, dispatch(): pl.pallas_call(functools.partial(dispatch_kernel, outer, inner, capacity)...  66 us
    all_to_all x2, waiting for transfers between devices, exchange(): lax.all_to_all(rows, 'expert', split_axis=0, concat_axis=0, tiled=True)  37 us
    broadcast_in_dim x3, other arithmetic, add_other_batch(): return total.astype(jnp.bfloat16)[None]  28.6 us
    dot_general x4, matrix products, contract_cols(): lax.dot_general(left, right, (((1,), (1,)), ((), ())), preferred_element_...  20.4 us
    dot_general x3, matrix products, contract_rows(): lax.dot_general(left, right, (((0,), (0,)), ((), ())), preferred_element_...  17.8 us
    all_to_all x2, starting transfers between devices, exchange(): lax.all_to_all(rows, 'expert', split_axis=0, concat_axis=0, tiled=True)  15.2 us
    dot_general x1, matrix products, body(): jnp.dot(up_rows, up_matrix, preferred_element_type=jnp.float32)  6.01 us
    dot_general x1, matrix products, body(): jnp.dot(gate_rows, gate_matrix, preferred_element_type=jnp.float32)  4.94 us
  transfers between devices with their start and end apart: 5, of which 2 were waited for; matrix products, arithmetic and copies ran while one was open for 34% of the time, Pallas kernels for 0%

profile of v2, /device:TPU:12, one launch (start us, length us, event | category | flops | bytes accessed | tf_op | source)
XLA Modules:
  0.0 213.8 jit_solution(12320655411829139574)
XLA Ops:
  2.0 0.9 copy-done
  2.9 0.9 copy-done.2
  3.9 66.0 %shard_map.118 = (bf16[512,2048]{1,0:T(8,128)(2,1)S(1)}, bf16[512,2048]{1,0:T(8,128)(2,1)S(1)}) custom-call(bf16[64,2048]{1,0:T(8,128)(2,1)S(1)} %copy-done.2, bf16[64,2048]{1,0:T(8,128)(2,1)S(1)} %copy-done, bf16[4,128,128]{2,1,0:T(8,128)(2,1)S(1)} %bitcast.78), custom_call_target="tpu_custom_call" | custom-call | tf_op jit(solution)/shard_map/pallas_call | solution.py:144
  69.9 1.3 copy-done.3
  71.3 6.0 %fusion.13 = f32[512,1408]{1,0:T(8,128)S(1)} fusion(bf16[512,2048]{1,0:T(8,128)(2,1)S(1)} %get-tuple-element.20, bf16[1,1408,2048]{2,1,0:T(8,128)(2,1)} %param.10), kind=kOutput, calls=%fused_computation.19 | convolution fusion | flops 2952790016 | bytes 10747904 | tf_op jit(solution)/shard_map/dot_general | solution.py:17
  77.3 5.2 %multiply_convert_fusion.2 = (bf16[512,1408]{1,0:T(8,128)(2,1)S(1)}, f32[512,1408]{1,0:T(8,128)}) fusion(f32[512,1408]{1,0:T(8,128)S(1)} %fusion.13, bf16[512,2048]{1,0:T(8,128)(2,1)S(1)} %get-tuple-element.20, bf16[1,1408,2048]{2,1,0:T(8,128)(2,1)S(1)} %bitcast.87), kind=kOutput, calls=%fused_computation.25 | convolution fusion | flops 2957115392 | bytes 15073280 | tf_op jit(solution)/shard_map/dot_general | solution.py:17
  82.5 4.6 %fusion.17 = bf16[512,2048]{1,0:T(8,128)(2,1)} fusion(bf16[512,1408]{1,0:T(8,128)(2,1)S(1)} %get-tuple-element.38, bf16[1,1408,2048]{2,1,0:T(8,128)(2,1)S(1)} %bitcast.85), kind=kOutput, calls=%fused_computation.22 | convolution fusion | flops 2953838592 | bytes 9306112 | tf_op jit(solution)/shard_map/dot_general | solution.py:201
  87.1 9.4 %all-to-all-start = ((bf16[16,32,2048]{2,1,0:T(8,128)(2,1)}), bf16[16,32,2048]{2,1,0:T(8,128)(2,1)}, u32[]{:S(2)}, u32[]{:S(2)}) async-start(bf16[16,32,2048]{2,1,0:T(8,128)(2,1)} %bitcast.83), calls=%async_computation | async-start | bytes 4194304 | tf_op jit(solution)/shard_map/all_to_all | solution.py:23
  96.6 7.9 %convolution_convert_fusion.2 = bf16[1408,2048]{1,0:T(8,128)(2,1)} fusion(bf16[512,1408]{1,0:T(8,128)(2,1)} %copy-done.11, bf16[512,2048]{1,0:T(8,128)(2,1)} %copy-done.3), kind=kOutput, calls=%fused_computation.5 | convolution fusion | flops 2955673600 | bytes 9306112 | tf_op jit(solution)/shard_map/dot_general | solution.py:11
  104.4 6.8 %multiply_convert_fusion = (bf16[512,1408]{1,0:T(8,128)(2,1)S(1)}, bf16[512,1408]{1,0:T(8,128)(2,1)S(1)}) fusion(f32[512,1408]{1,0:T(8,128)S(1)} %copy-done.7, f32[512,1408]{1,0:T(8,128)S(1)} %copy-done.12, bf16[512,2048]{1,0:T(8,128)(2,1)S(1)} %copy-done.4, bf16[1,1408,2048]{2,1,0:T(8,128)(2,1)} %param.12), kind=kOutput, calls=%fused_computation.23 | convolution fusion | flops 2962161664 | bytes 16515072 | tf_op jit(solution)/shard_map/dot_general | solution.py:17
  111.2 5.0 %convolution_convert_fusion = bf16[1408,2048]{1,0:T(8,128)(2,1)} fusion(bf16[512,1408]{1,0:T(8,128)(2,1)S(1)} %get-tuple-element.26, bf16[512,2048]{1,0:T(8,128)(2,1)S(1)} %get-tuple-element.20), kind=kOutput, calls=%fused_computation.3 | convolution fusion | flops 2955673600 | bytes 9306112 | tf_op jit(solution)/shard_map/dot_general | solution.py:11
  116.2 5.0 %convolution_convert_fusion.1 = bf16[1408,2048]{1,0:T(8,128)(2,1)} fusion(bf16[512,1408]{1,0:T(8,128)(2,1)S(1)} %get-tuple-element.25, bf16[512,2048]{1,0:T(8,128)(2,1)S(1)} %get-tuple-element.20), kind=kOutput, calls=%fused_computation.4 | convolution fusion | flops 2955673600 | bytes 9306112 | tf_op jit(solution)/shard_map/dot_general | solution.py:11
  121.2 22.7 %all-to-all-done = bf16[16,32,2048]{2,1,0:T(8,128)(2,1)} async-done(((bf16[16,32,2048]{2,1,0:T(8,128)(2,1)}), bf16[16,32,2048]{2,1,0:T(8,128)(2,1)}, u32[]{:S(2)}, u32[]{:S(2)}) %all-to-all-start) | async-done | bytes 2097184 | tf_op jit(solution)/shard_map/all_to_all | solution.py:23
  144.7 2.5 %convolution_bitcast_fusion = f32[64,512]{1,0:T(8,128)S(1)} fusion(bf16[512,2048]{1,0:T(8,128)(2,1)} %bitcast.8, bf16[64,2048]{1,0:T(8,128)(2,1)S(1)} %copy-done.1), kind=kOutput, calls=%fused_computation.31 | convolution fusion | flops 134217728 | bytes 2490368 | tf_op jit(solution)/shard_map/dot_general | solution.py:17
  147.3 6.0 %fusion.7 = f32[512,2048]{1,0:T(8,128)S(1)} fusion(bf16[512,1408]{1,0:T(8,128)(2,1)} %copy-done.10, bf16[1,1408,2048]{2,1,0:T(8,128)(2,1)} %param.11), kind=kOutput, calls=%fused_computation.13 | convolution fusion | flops 2952790016 | bytes 11403264 | tf_op jit(solution)/shard_map/dot_general | solution.py:221
  153.4 4.9 %add_convert_fusion.3 = bf16[512,2048]{1,0:T(8,128)(2,1)} fusion(f32[512,2048]{1,0:T(8,128)S(1)} %fusion.7, bf16[512,1408]{1,0:T(8,128)(2,1)S(1)} %copy-done.9, bf16[1,1408,2048]{2,1,0:T(8,128)(2,1)S(1)} %bitcast.89), kind=kOutput, calls=%fused_computation.21 | convolution fusion | flops 2954887168 | bytes 13500416 | tf_op jit(solution)/shard_map/dot_general | solution.py:220
  158.3 5.8 %all-to-all-start.1 = ((bf16[16,32,2048]{2,1,0:T(8,128)(2,1)}), bf16[16,32,2048]{2,1,0:T(8,128)(2,1)S(1)}, u32[]{:S(2)}, u32[]{:S(2)}) async-start(bf16[16,32,2048]{2,1,0:T(8,128)(2,1)} %bitcast.82), calls=%async_computation.1 | async-start | bytes 4194304 | tf_op jit(solution)/shard_map/all_to_all | solution.py:23
  164.7 2.1 fusion.26
  166.8 2.8 %fusion.21 = bf16[64,2048]{1,0:T(8,128)(2,1)} fusion(f32[64,2048]{1,0:T(8,128)S(1)} %fusion.26, bf16[64,512]{0,1:T(8,128)(2,1)S(1)} %fusion.24, bf16[512,2048]{1,0:T(8,128)(2,1)} %bitcast.8), kind=kOutput, calls=%fused_computation.29 | convolution fusion | flops 134479872 | bytes 2949120 | tf_op jit(solution)/shard_map/dot_general | solution.py:227
  169.6 10.4 %fusion = bf16[1,1408,2048]{2,1,0:T(8,128)(2,1)} fusion(bf16[1408,2048]{1,0:T(8,128)(2,1)} %collective-permute-done, bf16[1408,2048]{1,0:T(8,128)(2,1)} %convolution_convert_fusion.1), kind=kLoop, calls=%fused_computation.6 | loop fusion | flops 11534336 | bytes 17301504 | tf_op jit(solution)/shard_map/broadcast_in_dim | solution.py:45
  180.0 10.3 %fusion.1 = bf16[1,1408,2048]{2,1,0:T(8,128)(2,1)} fusion(bf16[1408,2048]{1,0:T(8,128)(2,1)} %collective-permute-done.1, bf16[1408,2048]{1,0:T(8,128)(2,1)} %convolution_convert_fusion), kind=kLoop, calls=%fused_computation.7 | loop fusion | flops 11534336 | bytes 17301504 | tf_op jit(solution)/shard_map/broadcast_in_dim | solution.py:45
  190.3 7.9 %fusion.2 = bf16[1,1408,2048]{2,1,0:T(8,128)(2,1)} fusion(bf16[1408,2048]{1,0:T(8,128)(2,1)} %collective-permute-done.2, bf16[1408,2048]{1,0:T(8,128)(2,1)S(1)} %bitcast.81), kind=kLoop, calls=%fused_computation.8 | loop fusion | flops 11534336 | bytes 17301504 | tf_op jit(solution)/shard_map/broadcast_in_dim | solution.py:45
  198.3 14.3 %all-to-all-done.1 = bf16[16,32,2048]{2,1,0:T(8,128)(2,1)S(1)} async-done(((bf16[16,32,2048]{2,1,0:T(8,128)(2,1)}), bf16[16,32,2048]{2,1,0:T(8,128)(2,1)S(1)}, u32[]{:S(2)}, u32[]{:S(2)}) %all-to-all-start.1) | async-done | bytes 2097184 | tf_op jit(solution)/shard_map/all_to_all | solution.py:23
  212.6 1.2 convolution_convert_fusion.3
  (60 shorter events, 2.9 us)
Async XLA Ops:
  3.9 73.4 %slice-start.4 = ((s8[5767168]{0:T(1024)(128)(4,1)}), s8[4194304]{0:T(1024)(128)(4,1)S(1)}, s32[]{:S(2)}) async-start(s8[5767168]{0:T(1024)(128)(4,1)} %bitcast.86), calls=%async_computation.6 | async-start | bytes 8388608
  69.9 1.3 copy-start.3
  71.2 6.0 %slice-start.5 = ((s8[5767168]{0:T(1024)(128)(4,1)}), s8[1572864]{0:T(1024)(128)(4,1)S(1)}, s32[]{:S(2)}) async-start(s8[5767168]{0:T(1024)(128)(4,1)} %bitcast.86), calls=%async_computation.7 | async-start | bytes 3145728
  71.3 11.2 %slice-start.2 = ((s8[5767168]{0:T(1024)(128)(4,1)}), s8[4194304]{0:T(1024)(128)(4,1)S(1)}, s32[]{:S(2)}) async-start(s8[5767168]{0:T(1024)(128)(4,1)} %bitcast.84), calls=%async_computation.4 | async-start | bytes 8388608
  77.3 5.2 %copy-start.6 = (f32[512,1408]{1,0:T(8,128)}, f32[512,1408]{1,0:T(8,128)S(1)}, u32[]{:S(2)}) copy-start(f32[512,1408]{1,0:T(8,128)S(1)} %fusion.13) | copy-start | bytes 8650756
  77.3 5.2 %slice-start.3 = ((s8[5767168]{0:T(1024)(128)(4,1)}), s8[1572864]{0:T(1024)(128)(4,1)S(1)}, s32[]{:S(2)}) async-start(s8[5767168]{0:T(1024)(128)(4,1)} %bitcast.84), calls=%async_computation.5 | async-start | bytes 3145728
  82.5 4.6 %copy-start.11 = (bf16[512,1408]{1,0:T(8,128)(2,1)}, bf16[512,1408]{1,0:T(8,128)(2,1)S(1)}, u32[]{:S(2)}) copy-start(bf16[512,1408]{1,0:T(8,128)(2,1)S(1)} %get-tuple-element.38) | copy-start | bytes 4325380
  87.1 56.8 %all-to-all-start = ((bf16[16,32,2048]{2,1,0:T(8,128)(2,1)}), bf16[16,32,2048]{2,1,0:T(8,128)(2,1)}, u32[]{:S(2)}, u32[]{:S(2)}) async-start(bf16[16,32,2048]{2,1,0:T(8,128)(2,1)} %bitcast.83), calls=%async_computation | async-start | bytes 4194304 | tf_op jit(solution)/shard_map/all_to_all | solution.py:23
  96.5 7.9 %copy-start.4 = (bf16[512,2048]{1,0:T(8,128)(2,1)S(1)}, bf16[512,2048]{1,0:T(8,128)(2,1)}, u32[]{:S(2)}) copy-start(bf16[512,2048]{1,0:T(8,128)(2,1)} %copy-done.3) | copy-start | bytes 6291460
  96.5 7.9 %copy-start.7 = (f32[512,1408]{1,0:T(8,128)S(1)}, f32[512,1408]{1,0:T(8,128)}, u32[]{:S(2)}) copy-start(f32[512,1408]{1,0:T(8,128)} %copy-done.6) | copy-start | bytes 8650756
  96.5 7.9 %copy-start.12 = (f32[512,1408]{1,0:T(8,128)S(1)}, f32[512,1408]{1,0:T(8,128)}, u32[]{:S(2)}) copy-start(f32[512,1408]{1,0:T(8,128)} %get-tuple-element.39) | copy-start | bytes 8650756
  111.2 5.0 %copy-start.10 = (bf16[512,1408]{1,0:T(8,128)(2,1)}, bf16[512,1408]{1,0:T(8,128)(2,1)S(1)}, u32[]{:S(2)}) copy-start(bf16[512,1408]{1,0:T(8,128)(2,1)S(1)} %get-tuple-element.26) | copy-start | bytes 4325380
  111.2 5.0 %copy-start.8 = (bf16[512,1408]{1,0:T(8,128)(2,1)}, bf16[512,1408]{1,0:T(8,128)(2,1)S(1)}, u32[]{:S(2)}) copy-start(bf16[512,1408]{1,0:T(8,128)(2,1)S(1)} %get-tuple-element.25) | copy-start | bytes 4325380
  116.2 28.4 %copy-start.1 = (bf16[64,2048]{1,0:T(8,128)(2,1)S(1)}, bf16[64,2048]{1,0:T(8,128)(2,1)}, u32[]{:S(2)}) copy-start(bf16[64,2048]{1,0:T(8,128)(2,1)} %g_ref.1) | copy-start | bytes 786436
  143.9 25.7 %collective-permute-start = (bf16[1408,2048]{1,0:T(8,128)(2,1)}, bf16[1408,2048]{1,0:T(8,128)(2,1)}, u32[]{:S(2)}, u32[]{:S(2)}) collective-permute-start(bf16[1408,2048]{1,0:T(8,128)(2,1)} %convolution_convert_fusion.1), channel_id=1, source_target_pairs={{0,16},{16,0},{1,17},{17,1},{2,18},{18,2},{3,19},{19,3},{4,20},{20... | collective-permute-start | bytes 17301512 | tf_op jit(solution)/shard_map/ppermute | solution.py:43
  143.9 36.1 %collective-permute-start.1 = (bf16[1408,2048]{1,0:T(8,128)(2,1)}, bf16[1408,2048]{1,0:T(8,128)(2,1)}, u32[]{:S(2)}, u32[]{:S(2)}) collective-permute-start(bf16[1408,2048]{1,0:T(8,128)(2,1)} %convolution_convert_fusion), channel_id=1, source_target_pairs={{0,16},{16,0},{1,17},{17,1},{2,18},{18,2},{3,19},{19,3},{4,20},{20... | collective-permute-start | bytes 17301512 | tf_op jit(solution)/shard_map/ppermute | solution.py:43
  144.6 45.8 %collective-permute-start.2 = (bf16[1408,2048]{1,0:T(8,128)(2,1)}, bf16[1408,2048]{1,0:T(8,128)(2,1)}, u32[]{:S(2)}, u32[]{:S(2)}) collective-permute-start(bf16[1408,2048]{1,0:T(8,128)(2,1)} %convolution_convert_fusion.2), channel_id=1, source_target_pairs={{0,16},{16,0},{1,17},{17,1},{2,18},{18,2},{3,19},{19,3},{4,20},{20... | collective-permute-start | bytes 17301512 | tf_op jit(solution)/shard_map/ppermute | solution.py:43
  144.7 8.7 %slice-start.6 = ((s8[5767168]{0:T(1024)(128)(4,1)}), s8[1572864]{0:T(1024)(128)(4,1)S(1)}, s32[]{:S(2)}) async-start(s8[5767168]{0:T(1024)(128)(4,1)} %bitcast.88), calls=%async_computation.8 | async-start | bytes 3145728
  147.3 6.1 %slice-start.7 = ((s8[5767168]{0:T(1024)(128)(4,1)}), s8[4194304]{0:T(1024)(128)(4,1)S(1)}, s32[]{:S(2)}) async-start(s8[5767168]{0:T(1024)(128)(4,1)} %bitcast.88), calls=%async_computation.9 | async-start | bytes 8388608
  147.3 6.0 %copy-start.9 = (bf16[512,1408]{1,0:T(8,128)(2,1)S(1)}, bf16[512,1408]{1,0:T(8,128)(2,1)}, u32[]{:S(2)}) copy-start(bf16[512,1408]{1,0:T(8,128)(2,1)} %copy-done.8) | copy-start | bytes 4325380
  158.3 5.8 %copy-start.5 = (s32[64,6]{0,1:T(8,128)S(1)}, s32[64,6]{0,1:T(8,128)}, u32[]{:S(2)}) copy-start(s32[64,6]{0,1:T(8,128)} %param.8) | copy-start | bytes 4612
  158.3 54.3 %all-to-all-start.1 = ((bf16[16,32,2048]{2,1,0:T(8,128)(2,1)}), bf16[16,32,2048]{2,1,0:T(8,128)(2,1)S(1)}, u32[]{:S(2)}, u32[]{:S(2)}) async-start(bf16[16,32,2048]{2,1,0:T(8,128)(2,1)} %bitcast.82), calls=%async_computation.1 | async-start | bytes 4194304 | tf_op jit(solution)/shard_map/all_to_all | solution.py:23
  169.6 20.7 %slice-start = ((s8[5767168]{0:T(1024)(128)(4,1)}), s8[4194304]{0:T(1024)(128)(4,1)S(1)}, s32[]{:S(2)}) async-start(s8[5767168]{0:T(1024)(128)(4,1)} %bitcast.80), calls=%async_computation.2 | async-start | bytes 8388608
  180.0 10.3 %slice-start.1 = ((s8[5767168]{0:T(1024)(128)(4,1)}), s8[1572864]{0:T(1024)(128)(4,1)S(1)}, s32[]{:S(2)}) async-start(s8[5767168]{0:T(1024)(128)(4,1)} %bitcast.80), calls=%async_computation.3 | async-start | bytes 3145728
  (2 other events, 1.9 us)

commit v3 on v2

--- a/solution.py
+++ b/solution.py
@@ -210,14 +210,15 @@
     down_term = contract_rows(hidden, expert_grads).astype(jnp.bfloat16)
     gate_term = contract_rows(gate_rows, expert_rows).astype(jnp.bfloat16)
     up_term = contract_rows(up_rows, expert_rows).astype(jnp.bfloat16)
-    gate_rows, up_rows, down_term, gate_term, up_term, returned = lax.optimization_barrier(
-        (gate_rows, up_rows, down_term, gate_term, up_term, returned)
+    gate_share = jnp.dot(gate_rows, gate_matrix, preferred_element_type=jnp.float32)
+    gate_share, up_rows, down_term, gate_term, up_term, returned = lax.optimization_barrier(
+        (gate_share, up_rows, down_term, gate_term, up_term, returned)
     )
     down_out = add_other_batch(down_term)
     gate_out = add_other_batch(gate_term)
     up_out = add_other_batch(up_term)
     grad_part = (
-        jnp.dot(gate_rows, gate_matrix, preferred_element_type=jnp.float32)
+        gate_share
         + jnp.dot(up_rows, up_matrix, preferred_element_type=jnp.float32)
     ).astype(jnp.bfloat16)
     returned_grads = exchange(scatter_features(grad_part))

time: 215 us -> 209 us (0.972)
  waiting for transfers between devices: 37 us -> 29.5 us
    all_to_all x2, waiting for transfers between devices: 37 us -> 29.5 us  [exchange(): lax.all_to_all(rows, 'expert', split_axis=0, concat_axis=0, tiled=True)]
  transfers between devices with their start and end apart: 5 -> 5, of which waited for: 2 -> 2; matrix products, arithmetic and copies ran while one was open for 34% -> 36% of each run, Pallas kernels for 0% -> 0%
where the time goes in v3:
time: 209 us; the launch traced here: 208 us
  Pallas kernels  66 us (32%)
  matrix products  62.1 us (30%)
  other arithmetic  30.5 us (15%)
  waiting for transfers between devices  29.5 us (14%)
  starting transfers between devices  15.7 us (8%)
  local copies, waits for them, and re-layouts  3.5 us (2%)
    pallas_call x1, Pallas kernels, dispatch(): pl.pallas_call(functools.partial(dispatch_kernel, outer, inner, capacity)...  66 us
    all_to_all x2, waiting for transfers between devices, exchange(): lax.all_to_all(rows, 'expert', split_axis=0, concat_axis=0, tiled=True)  29.5 us
    broadcast_in_dim x3, other arithmetic, add_other_batch(): return total.astype(jnp.bfloat16)[None]  28.6 us
    dot_general x4, matrix products, contract_cols(): lax.dot_general(left, right, (((1,), (1,)), ((), ())), preferred_element_...  20.3 us
    dot_general x3, matrix products, contract_rows(): lax.dot_general(left, right, (((0,), (0,)), ((), ())), preferred_element_...  17.8 us
    all_to_all x2, starting transfers between devices, exchange(): lax.all_to_all(rows, 'expert', split_axis=0, concat_axis=0, tiled=True)  15.2 us
    dot_general x1, matrix products, body(): jnp.dot(up_rows, up_matrix, preferred_element_type=jnp.float32)  8.11 us
    dot_general x1, matrix products, body(): jnp.dot(gate_rows, gate_matrix, preferred_element_type=jnp.float32)  5.03 us
  transfers between devices with their start and end apart: 5, of which 2 were waited for; matrix products, arithmetic and copies ran while one was open for 36% of the time, Pallas kernels for 0%

profile of v3, /device:TPU:12, one launch (start us, length us, event | category | flops | bytes accessed | tf_op | source)
XLA Modules:
  0.0 208.2 jit_solution(17667264222802249492)
XLA Ops:
  2.0 0.9 copy-done
  2.9 0.9 copy-done.2
  3.9 66.0 %shard_map.118 = (bf16[512,2048]{1,0:T(8,128)(2,1)S(1)}, bf16[512,2048]{1,0:T(8,128)(2,1)S(1)}) custom-call(bf16[64,2048]{1,0:T(8,128)(2,1)S(1)} %copy-done.2, bf16[64,2048]{1,0:T(8,128)(2,1)S(1)} %copy-done, bf16[4,128,128]{2,1,0:T(8,128)(2,1)S(1)} %bitcast.78), custom_call_target="tpu_custom_call" | custom-call | tf_op jit(solution)/shard_map/pallas_call | solution.py:144
  69.9 1.3 copy-done.3
  71.2 6.0 %fusion.13 = f32[512,1408]{1,0:T(8,128)S(1)} fusion(bf16[512,2048]{1,0:T(8,128)(2,1)S(1)} %get-tuple-element.20, bf16[1,1408,2048]{2,1,0:T(8,128)(2,1)} %param.10), kind=kOutput, calls=%fused_computation.19 | convolution fusion | flops 2952790016 | bytes 10747904 | tf_op jit(solution)/shard_map/dot_general | solution.py:17
  77.3 5.2 %multiply_convert_fusion.2 = (bf16[512,1408]{1,0:T(8,128)(2,1)S(1)}, f32[512,1408]{1,0:T(8,128)}) fusion(f32[512,1408]{1,0:T(8,128)S(1)} %fusion.13, bf16[512,2048]{1,0:T(8,128)(2,1)S(1)} %get-tuple-element.20, bf16[1,1408,2048]{2,1,0:T(8,128)(2,1)S(1)} %bitcast.89), kind=kOutput, calls=%fused_computation.25 | convolution fusion | flops 2957115392 | bytes 15073280 | tf_op jit(solution)/shard_map/dot_general | solution.py:17
  82.5 4.7 %fusion.17 = bf16[512,2048]{1,0:T(8,128)(2,1)} fusion(bf16[512,1408]{1,0:T(8,128)(2,1)S(1)} %get-tuple-element.38, bf16[1,1408,2048]{2,1,0:T(8,128)(2,1)S(1)} %bitcast.85), kind=kOutput, calls=%fused_computation.22 | convolution fusion | flops 2953838592 | bytes 9306112 | tf_op jit(solution)/shard_map/dot_general | solution.py:201
  87.1 9.4 %all-to-all-start = ((bf16[16,32,2048]{2,1,0:T(8,128)(2,1)}), bf16[16,32,2048]{2,1,0:T(8,128)(2,1)}, u32[]{:S(2)}, u32[]{:S(2)}) async-start(bf16[16,32,2048]{2,1,0:T(8,128)(2,1)} %bitcast.83), calls=%async_computation | async-start | bytes 4194304 | tf_op jit(solution)/shard_map/all_to_all | solution.py:23
  96.6 7.9 %convolution_convert_fusion.2 = bf16[1408,2048]{1,0:T(8,128)(2,1)} fusion(bf16[512,1408]{1,0:T(8,128)(2,1)} %copy-done.10, bf16[512,2048]{1,0:T(8,128)(2,1)} %copy-done.3), kind=kOutput, calls=%fused_computation.5 | convolution fusion | flops 2955673600 | bytes 9306112 | tf_op jit(solution)/shard_map/dot_general | solution.py:11
  104.5 6.8 %multiply_convert_fusion = (bf16[512,1408]{1,0:T(8,128)(2,1)S(1)}, bf16[512,1408]{1,0:T(8,128)(2,1)S(1)}) fusion(f32[512,1408]{1,0:T(8,128)S(1)} %copy-done.7, f32[512,1408]{1,0:T(8,128)S(1)} %copy-done.11, bf16[512,2048]{1,0:T(8,128)(2,1)S(1)} %copy-done.4, bf16[1,1408,2048]{2,1,0:T(8,128)(2,1)} %param.12), kind=kOutput, calls=%fused_computation.23 | convolution fusion | flops 2962161664 | bytes 16515072 | tf_op jit(solution)/shard_map/dot_general | solution.py:17
  111.3 5.0 %convolution_convert_fusion.1 = bf16[1408,2048]{1,0:T(8,128)(2,1)} fusion(bf16[512,1408]{1,0:T(8,128)(2,1)S(1)} %get-tuple-element.37, bf16[512,2048]{1,0:T(8,128)(2,1)S(1)} %get-tuple-element.20), kind=kOutput, calls=%fused_computation.4 | convolution fusion | flops 2955673600 | bytes 9306112 | tf_op jit(solution)/shard_map/dot_general | solution.py:11
  116.2 5.0 %convolution_convert_fusion = bf16[1408,2048]{1,0:T(8,128)(2,1)} fusion(bf16[512,1408]{1,0:T(8,128)(2,1)S(1)} %get-tuple-element.26, bf16[512,2048]{1,0:T(8,128)(2,1)S(1)} %get-tuple-element.20), kind=kOutput, calls=%fused_computation.3 | convolution fusion | flops 2955673600 | bytes 9306112 | tf_op jit(solution)/shard_map/dot_general | solution.py:11
  121.2 5.0 %fusion.11 = f32[512,2048]{1,0:T(8,128)} fusion(bf16[512,1408]{1,0:T(8,128)(2,1)S(1)} %get-tuple-element.37, bf16[1,1408,2048]{2,1,0:T(8,128)(2,1)S(1)} %bitcast.87), kind=kOutput, calls=%fused_computation.17 | convolution fusion | flops 2952790016 | bytes 11403264 | tf_op jit(solution)/shard_map/dot_general | solution.py:213
  126.3 17.7 %all-to-all-done = bf16[16,32,2048]{2,1,0:T(8,128)(2,1)} async-done(((bf16[16,32,2048]{2,1,0:T(8,128)(2,1)}), bf16[16,32,2048]{2,1,0:T(8,128)(2,1)}, u32[]{:S(2)}, u32[]{:S(2)}) %all-to-all-start) | async-done | bytes 2097184 | tf_op jit(solution)/shard_map/all_to_all | solution.py:23
  144.6 8.1 %add_convert_fusion.3 = bf16[512,2048]{1,0:T(8,128)(2,1)} fusion(f32[512,2048]{1,0:T(8,128)} %fusion.11, bf16[512,1408]{1,0:T(8,128)(2,1)S(1)} %copy-done.9, bf16[1,1408,2048]{2,1,0:T(8,128)(2,1)} %param.11), kind=kOutput, calls=%fused_computation.21 | convolution fusion | flops 2954887168 | bytes 13500416 | tf_op jit(solution)/shard_map/dot_general | solution.py:222
  152.7 5.8 %all-to-all-start.1 = ((bf16[16,32,2048]{2,1,0:T(8,128)(2,1)}), bf16[16,32,2048]{2,1,0:T(8,128)(2,1)S(1)}, u32[]{:S(2)}, u32[]{:S(2)}) async-start(bf16[16,32,2048]{2,1,0:T(8,128)(2,1)} %bitcast.82), calls=%async_computation.1 | async-start | bytes 4194304 | tf_op jit(solution)/shard_map/all_to_all | solution.py:23
  158.5 2.3 %convolution_bitcast_fusion = f32[64,512]{1,0:T(8,128)S(1)} fusion(bf16[512,2048]{1,0:T(8,128)(2,1)} %bitcast.8, bf16[64,2048]{1,0:T(8,128)(2,1)S(1)} %copy-done.1), kind=kOutput, calls=%fused_computation.31 | convolution fusion | flops 134217728 | bytes 2490368 | tf_op jit(solution)/shard_map/dot_general | solution.py:17
  161.7 2.1 %fusion.26 = f32[64,2048]{1,0:T(8,128)S(1)} fusion(bf16[64,512]{0,1:T(8,128)(2,1)S(1)} %fusion.23, bf16[512,2048]{1,0:T(8,128)(2,1)} %bitcast.8), kind=kOutput, calls=%fused_computation.47 | convolution fusion | flops 134217728 | bytes 2686976 | tf_op jit(solution)/shard_map/dot_general | solution.py:227
  163.8 2.8 %fusion.21 = bf16[64,2048]{1,0:T(8,128)(2,1)} fusion(f32[64,2048]{1,0:T(8,128)S(1)} %fusion.26, bf16[64,512]{0,1:T(8,128)(2,1)S(1)} %fusion.24, bf16[512,2048]{1,0:T(8,128)(2,1)} %bitcast.8), kind=kOutput, calls=%fused_computation.29 | convolution fusion | flops 134479872 | bytes 2949120 | tf_op jit(solution)/shard_map/dot_general | solution.py:228
  166.6 10.4 %fusion = bf16[1,1408,2048]{2,1,0:T(8,128)(2,1)} fusion(bf16[1408,2048]{1,0:T(8,128)(2,1)} %collective-permute-done, bf16[1408,2048]{1,0:T(8,128)(2,1)} %convolution_convert_fusion.1), kind=kLoop, calls=%fused_computation.6 | loop fusion | flops 11534336 | bytes 17301504 | tf_op jit(solution)/shard_map/broadcast_in_dim | solution.py:45
  177.0 10.3 %fusion.1 = bf16[1,1408,2048]{2,1,0:T(8,128)(2,1)} fusion(bf16[1408,2048]{1,0:T(8,128)(2,1)} %collective-permute-done.1, bf16[1408,2048]{1,0:T(8,128)(2,1)} %convolution_convert_fusion), kind=kLoop, calls=%fused_computation.7 | loop fusion | flops 11534336 | bytes 17301504 | tf_op jit(solution)/shard_map/broadcast_in_dim | solution.py:45
  187.3 7.9 %fusion.2 = bf16[1,1408,2048]{2,1,0:T(8,128)(2,1)} fusion(bf16[1408,2048]{1,0:T(8,128)(2,1)} %collective-permute-done.2, bf16[1408,2048]{1,0:T(8,128)(2,1)S(1)} %bitcast.81), kind=kLoop, calls=%fused_computation.8 | loop fusion | flops 11534336 | bytes 17301504 | tf_op jit(solution)/shard_map/broadcast_in_dim | solution.py:45
  195.2 11.8 %all-to-all-done.1 = bf16[16,32,2048]{2,1,0:T(8,128)(2,1)S(1)} async-done(((bf16[16,32,2048]{2,1,0:T(8,128)(2,1)}), bf16[16,32,2048]{2,1,0:T(8,128)(2,1)S(1)}, u32[]{:S(2)}, u32[]{:S(2)}) %all-to-all-start.1) | async-done | bytes 2097184 | tf_op jit(solution)/shard_map/all_to_all | solution.py:23
  207.0 1.2 convolution_convert_fusion.3
  (58 shorter events, 2.9 us)
Async XLA Ops:
  2.0 1.0 copy-start
  3.9 73.3 %slice-start.6 = ((s8[5767168]{0:T(1024)(128)(4,1)}), s8[4194304]{0:T(1024)(128)(4,1)S(1)}, s32[]{:S(2)}) async-start(s8[5767168]{0:T(1024)(128)(4,1)} %bitcast.88), calls=%async_computation.8 | async-start | bytes 8388608
  69.9 1.3 copy-start.3
  71.2 6.0 %slice-start.7 = ((s8[5767168]{0:T(1024)(128)(4,1)}), s8[1572864]{0:T(1024)(128)(4,1)S(1)}, s32[]{:S(2)}) async-start(s8[5767168]{0:T(1024)(128)(4,1)} %bitcast.88), calls=%async_computation.9 | async-start | bytes 3145728
  71.2 11.2 %slice-start.2 = ((s8[5767168]{0:T(1024)(128)(4,1)}), s8[4194304]{0:T(1024)(128)(4,1)S(1)}, s32[]{:S(2)}) async-start(s8[5767168]{0:T(1024)(128)(4,1)} %bitcast.84), calls=%async_computation.4 | async-start | bytes 8388608
  77.2 5.2 %copy-start.6 = (f32[512,1408]{1,0:T(8,128)}, f32[512,1408]{1,0:T(8,128)S(1)}, u32[]{:S(2)}) copy-start(f32[512,1408]{1,0:T(8,128)S(1)} %fusion.13) | copy-start | bytes 8650756
  77.3 5.2 %slice-start.3 = ((s8[5767168]{0:T(1024)(128)(4,1)}), s8[1572864]{0:T(1024)(128)(4,1)S(1)}, s32[]{:S(2)}) async-start(s8[5767168]{0:T(1024)(128)(4,1)} %bitcast.84), calls=%async_computation.5 | async-start | bytes 3145728
  82.4 4.7 %copy-start.10 = (bf16[512,1408]{1,0:T(8,128)(2,1)}, bf16[512,1408]{1,0:T(8,128)(2,1)S(1)}, u32[]{:S(2)}) copy-start(bf16[512,1408]{1,0:T(8,128)(2,1)S(1)} %get-tuple-element.38) | copy-start | bytes 4325380
  87.1 56.8 %all-to-all-start = ((bf16[16,32,2048]{2,1,0:T(8,128)(2,1)}), bf16[16,32,2048]{2,1,0:T(8,128)(2,1)}, u32[]{:S(2)}, u32[]{:S(2)}) async-start(bf16[16,32,2048]{2,1,0:T(8,128)(2,1)} %bitcast.83), calls=%async_computation | async-start | bytes 4194304 | tf_op jit(solution)/shard_map/all_to_all | solution.py:23
  96.6 7.9 %copy-start.4 = (bf16[512,2048]{1,0:T(8,128)(2,1)S(1)}, bf16[512,2048]{1,0:T(8,128)(2,1)}, u32[]{:S(2)}) copy-start(bf16[512,2048]{1,0:T(8,128)(2,1)} %copy-done.3) | copy-start | bytes 6291460
  96.6 7.9 %copy-start.7 = (f32[512,1408]{1,0:T(8,128)S(1)}, f32[512,1408]{1,0:T(8,128)}, u32[]{:S(2)}) copy-start(f32[512,1408]{1,0:T(8,128)} %copy-done.6) | copy-start | bytes 8650756
  96.6 7.9 %copy-start.11 = (f32[512,1408]{1,0:T(8,128)S(1)}, f32[512,1408]{1,0:T(8,128)}, u32[]{:S(2)}) copy-start(f32[512,1408]{1,0:T(8,128)} %get-tuple-element.39) | copy-start | bytes 8650756
  111.2 5.0 %copy-start.8 = (bf16[512,1408]{1,0:T(8,128)(2,1)}, bf16[512,1408]{1,0:T(8,128)(2,1)S(1)}, u32[]{:S(2)}) copy-start(bf16[512,1408]{1,0:T(8,128)(2,1)S(1)} %get-tuple-element.26) | copy-start | bytes 4325380
  111.2 10.0 %slice-start.4 = ((s8[5767168]{0:T(1024)(128)(4,1)}), s8[4194304]{0:T(1024)(128)(4,1)S(1)}, s32[]{:S(2)}) async-start(s8[5767168]{0:T(1024)(128)(4,1)} %bitcast.86), calls=%async_computation.6 | async-start | bytes 8388608
  116.2 5.0 %slice-start.5 = ((s8[5767168]{0:T(1024)(128)(4,1)}), s8[1572864]{0:T(1024)(128)(4,1)S(1)}, s32[]{:S(2)}) async-start(s8[5767168]{0:T(1024)(128)(4,1)} %bitcast.86), calls=%async_computation.7 | async-start | bytes 3145728
  121.2 23.4 %copy-start.9 = (bf16[512,1408]{1,0:T(8,128)(2,1)S(1)}, bf16[512,1408]{1,0:T(8,128)(2,1)}, u32[]{:S(2)}) copy-start(bf16[512,1408]{1,0:T(8,128)(2,1)} %copy-done.8) | copy-start | bytes 4325380
  144.0 22.6 %collective-permute-start = (bf16[1408,2048]{1,0:T(8,128)(2,1)}, bf16[1408,2048]{1,0:T(8,128)(2,1)}, u32[]{:S(2)}, u32[]{:S(2)}) collective-permute-start(bf16[1408,2048]{1,0:T(8,128)(2,1)} %convolution_convert_fusion.1), channel_id=1, source_target_pairs={{0,16},{16,0},{1,17},{17,1},{2,18},{18,2},{3,19},{19,3},{4,20},{20... | collective-permute-start | bytes 17301512 | tf_op jit(solution)/shard_map/ppermute | solution.py:43
  144.0 33.0 %collective-permute-start.1 = (bf16[1408,2048]{1,0:T(8,128)(2,1)}, bf16[1408,2048]{1,0:T(8,128)(2,1)}, u32[]{:S(2)}, u32[]{:S(2)}) collective-permute-start(bf16[1408,2048]{1,0:T(8,128)(2,1)} %convolution_convert_fusion), channel_id=1, source_target_pairs={{0,16},{16,0},{1,17},{17,1},{2,18},{18,2},{3,19},{19,3},{4,20},{20... | collective-permute-start | bytes 17301512 | tf_op jit(solution)/shard_map/ppermute | solution.py:43
  144.5 42.8 %collective-permute-start.2 = (bf16[1408,2048]{1,0:T(8,128)(2,1)}, bf16[1408,2048]{1,0:T(8,128)(2,1)}, u32[]{:S(2)}, u32[]{:S(2)}) collective-permute-start(bf16[1408,2048]{1,0:T(8,128)(2,1)} %convolution_convert_fusion.2), channel_id=1, source_target_pairs={{0,16},{16,0},{1,17},{17,1},{2,18},{18,2},{3,19},{19,3},{4,20},{20... | collective-permute-start | bytes 17301512 | tf_op jit(solution)/shard_map/ppermute | solution.py:43
  152.7 5.8 %copy-start.1 = (bf16[64,2048]{1,0:T(8,128)(2,1)S(1)}, bf16[64,2048]{1,0:T(8,128)(2,1)}, u32[]{:S(2)}) copy-start(bf16[64,2048]{1,0:T(8,128)(2,1)} %g_ref.1) | copy-start | bytes 786436
  152.7 8.3 %copy-start.5 = (s32[64,6]{0,1:T(8,128)S(1)}, s32[64,6]{0,1:T(8,128)}, u32[]{:S(2)}) copy-start(s32[64,6]{0,1:T(8,128)} %param.8) | copy-start | bytes 4612
  152.7 54.3 %all-to-all-start.1 = ((bf16[16,32,2048]{2,1,0:T(8,128)(2,1)}), bf16[16,32,2048]{2,1,0:T(8,128)(2,1)S(1)}, u32[]{:S(2)}, u32[]{:S(2)}) async-start(bf16[16,32,2048]{2,1,0:T(8,128)(2,1)} %bitcast.82), calls=%async_computation.1 | async-start | bytes 4194304 | tf_op jit(solution)/shard_map/all_to_all | solution.py:23
  166.6 20.7 %slice-start = ((s8[5767168]{0:T(1024)(128)(4,1)}), s8[4194304]{0:T(1024)(128)(4,1)S(1)}, s32[]{:S(2)}) async-start(s8[5767168]{0:T(1024)(128)(4,1)} %bitcast.80), calls=%async_computation.2 | async-start | bytes 8388608
  177.0 10.3 %slice-start.1 = ((s8[5767168]{0:T(1024)(128)(4,1)}), s8[1572864]{0:T(1024)(128)(4,1)S(1)}, s32[]{:S(2)}) async-start(s8[5767168]{0:T(1024)(128)(4,1)} %bitcast.80), calls=%async_computation.3 | async-start | bytes 3145728
  (1 other events, 0.9 us)
